TPU v7x, 512 devices: a whole 4x8x8 slice. The times are simulated.
512 devices in a mesh: chan: 16 (over y, z_lo), tm: 32 (over x, z_hi, core).
Axes of the slice: x: 4, y: 8, z: 8 (z_hi: 4, z_lo: 2; z = z_hi * 2 + z_lo), core: 2. Of those that a mesh axis runs over, the one named last changes fastest.
Arguments:
- spectra: bfloat16 [32, 512, 2, 2048], P('tm', 'chan'), may hold values from -420 to 420
- window_valid: int32 [32], P('tm'), may hold values 0 or 1
- pair_code: int32 [16, 32], P('chan'), may hold values from 0 to 143, as said below
- block_owner: int32 [16, 32], P('chan'), may hold values from 0 to 31, as said below
Outputs:
- stacks: float32 [16, 64, 8, 2048], P('chan', 'tm')
Inputs may be any that keep to these rules, and one draw needn't show every extreme that they name: `pair_code`: each code is r * 9 * 4 + d * 4 + s with r, s < 4 and d < 9; the 32 codes of a group are distinct. `block_owner`: no index keeps more than 2 blocks of one group.
All inputs are finite; a program needn't handle non-finite values. No bound on the sum of `window_valid` on one device may be relied on, other than what follows from the above.
Results may differ from a plain program's by a relative error of at most 0.0021.
Values may be sent and summed in bfloat16 or wider, within the bound.
No kernel may reach another device: no remote copies, remote signals or barrier semaphores. Data moves between devices by JAX's collectives and lax.ppermute only.
A program may use at most 64 MiB of HBM per device.

v0:
```python
import math

import jax
import jax.numpy as jnp
from jax import lax
from jax.sharding import PartitionSpec as P

CB = 8
G = 4
LAGS = 256
SLOTS = 2


EPS = 1e-05


def shifted(block, axis, distance):
    devices = range(lax.axis_size(axis))
    route = [((i - distance) % len(devices), i) for i in devices]
    return lax.ppermute(block, axis, route)


def lag_tables(freq_bins, lag_count):
    freq_index = jnp.arange(freq_bins, dtype=jnp.int32)[:, None]
    shifts = jnp.arange(lag_count, dtype=jnp.int32)[None, :] - lag_count // 2
    phase_int = freq_index * shifts % (2 * freq_bins)
    angles = phase_int.astype(jnp.float32) * (math.pi / freq_bins)
    return (jnp.cos(angles), -jnp.sin(angles))


def local(spectra, window_valid, pair_code, block_owner):
    windows, channels, _, freq_bins = spectra.shape
    groups_half = lax.axis_size("chan") // 2
    dist_count = groups_half + 1
    blocks = pair_code.shape[1]
    high = lax.Precision.HIGHEST
    raw_values = spectra.astype(jnp.float32)
    mean_power = jnp.mean(raw_values * raw_values, axis=(2, 3), keepdims=True)
    white = (raw_values * lax.rsqrt(mean_power + EPS)).astype(jnp.bfloat16)
    white_blocks = white.reshape(windows, G, CB, 2, freq_bins).transpose(1, 0, 2, 3, 4)
    weighted = white_blocks * window_valid.astype(jnp.bfloat16)[None, :, None, None, None]
    block_codes = pair_code[0]
    near_blk = block_codes // (dist_count * G)
    dist_blk = block_codes // G % dist_count
    far_blk = block_codes % G
    far_index = dist_blk * G + far_blk
    cos_table, sin_table = lag_tables(freq_bins, LAGS)
    joint_table = jnp.concatenate([cos_table, sin_table], axis=0)
    lag_scale = 1.0 / math.sqrt(freq_bins * windows * lax.axis_size("tm"))
    arrivals = [white_blocks]
    current = white_blocks
    for dist_now in range(1, groups_half + 1):
        current = shifted(current, "chan", -1)
        arrivals.append(current)
    arrived = jnp.stack(arrivals).reshape(dist_count * G, windows, CB, 2, freq_bins)
    step_blocks = math.gcd(blocks, 8)

    def block_group(group_start):
        start = group_start * step_blocks
        near_rows = lax.dynamic_slice_in_dim(near_blk, start, step_blocks, 0)
        far_rows = lax.dynamic_slice_in_dim(far_index, start, step_blocks, 0)
        near_side = jnp.take(weighted, near_rows, axis=0).astype(jnp.float32)
        far_side = jnp.take(arrived, far_rows, axis=0).astype(jnp.float32)
        near_re = near_side[:, :, :, 0][:, :, :, None, :]
        near_im = near_side[:, :, :, 1][:, :, :, None, :]
        far_re = far_side[:, :, :, 0][:, :, None, :, :]
        far_im = far_side[:, :, :, 1][:, :, None, :, :]
        real_part = jnp.sum(near_re * far_re + near_im * far_im, axis=1)
        imag_part = jnp.sum(near_im * far_re - near_re * far_im, axis=1)
        joined = jnp.concatenate([real_part, imag_part], axis=-1).reshape(
            step_blocks * CB * CB, 2 * freq_bins
        )
        lagged = jnp.dot(joined, joint_table, precision=high, preferred_element_type=jnp.float32)
        return (lagged * lag_scale).reshape(step_blocks, CB * CB * LAGS)

    grouped = lax.map(block_group, jnp.arange(blocks // step_blocks, dtype=jnp.int32))
    flat_stack = grouped.reshape(blocks, CB * CB * LAGS)
    owners = block_owner[0]
    order_index = jnp.arange(blocks, dtype=jnp.int32)
    earlier = order_index[None, :] < order_index[:, None]
    same_owner = owners[None, :] == owners[:, None]
    slot_rank = jnp.sum((earlier & same_owner).astype(jnp.int32), axis=1)
    totals = lax.psum(flat_stack, "tm")
    here = lax.axis_index("tm")
    slot_ids = jnp.arange(SLOTS, dtype=jnp.int32)
    picker = ((owners[None, :] == here) & (slot_rank[None, :] == slot_ids[:, None])).astype(
        jnp.float32
    )
    mine = jnp.dot(picker, totals, precision=high, preferred_element_type=jnp.float32)
    return mine.reshape(1, SLOTS, CB, CB * LAGS)


def solution(mesh):
    return jax.shard_map(
        local,
        mesh=mesh,
        in_specs=(P("tm", "chan", None, None), P("tm"), P("chan", None), P("chan", None)),
        out_specs=P("chan", "tm", None, None),
        check_vma=False,
    )
```

profile of v0, /device:TPU:1, one launch (start us, length us, event | category | flops | bytes accessed | tf_op | source)
XLA Modules:
  0.0 488.4 jit_solution(13042996622834384129)
XLA Ops:
  6.5 1.4 fusion.17
  7.9 1.2 fusion.18
  9.1 7.7 %collective-permute-start = (bf16[4,1,8,2,2048]{4,3,2,1,0:T(2,128)(2,1)S(1)}, bf16[4,1,8,2,2048]{4,3,2,1,0:T(2,128)(2,1)S(1)}, u32[]{:S(2)}, u32[]{:S(2)}) collective-permute-start(bf16[4,1,8,2,2048]{4,3,2,1,0:T(2,128)(2,1)S(1)} %bitcast.107), channel_id=1, source_target_pairs={{32,0},{64,32},{96,64},{128,96},{160,128},{192,160},{224,192},{256... | collective-permute-start | bytes 786440 | tf_op jit(solution)/shard_map/ppermute | solution.py:20
  16.9 8.2 %fusion.16 = (f32[2048,256]{1,0:T(8,128)S(1)}, f32[2048,256]{1,0:T(8,128)S(1)}) fusion(s32[256]{0:T(256)S(1)} %iota_add_fusion), kind=kLoop, calls=%fused_computation.36 | loop fusion | flops 7864320 | bytes 4195328 | tf_op jit(solution)/shard_map/cos | solution.py:28
  25.8 2.2 pad_maximum_fusion
  28.3 1.9 collective-permute-start.1
  30.5 6.5 %collective-permute-done.1 = bf16[4,1,8,2,2048]{4,3,2,1,0:T(2,128)(2,1)S(1)} collective-permute-done((bf16[4,1,8,2,2048]{4,3,2,1,0:T(2,128)(2,1)S(1)}, bf16[4,1,8,2,2048]{4,3,2,1,0:T(2,128)(2,1)S(1)}, u32[]{:S(2)}, u32[]{:S(2)}) %collective-permute-start.1) | collective-permute-done | bytes 262176 | tf_op jit(solution)/shard_map/ppermute | solution.py:20
  36.9 4.3 collective-permute-start.2
  41.5 3.7 collective-permute-done.2
  45.2 6.2 %collective-permute-start.3 = (bf16[4,1,8,2,2048]{4,3,2,1,0:T(2,128)(2,1)S(1)}, bf16[4,1,8,2,2048]{4,3,2,1,0:T(2,128)(2,1)S(1)}, u32[]{:S(2)}, u32[]{:S(2)}) collective-permute-start(bf16[4,1,8,2,2048]{4,3,2,1,0:T(2,128)(2,1)S(1)} %collective-permute-done.2), channel_id=1, source_target_pairs={{32,0},{64,32},{96,64},{128,96},{160,128},{192,160},{224,192},{256... | collective-permute-start | bytes 786440 | tf_op jit(solution)/shard_map/ppermute | solution.py:20
  51.6 3.1 collective-permute-done.3
  54.7 5.9 %collective-permute-start.4 = (bf16[4,1,8,2,2048]{4,3,2,1,0:T(2,128)(2,1)S(1)}, bf16[4,1,8,2,2048]{4,3,2,1,0:T(2,128)(2,1)S(1)}, u32[]{:S(2)}, u32[]{:S(2)}) collective-permute-start(bf16[4,1,8,2,2048]{4,3,2,1,0:T(2,128)(2,1)S(1)} %collective-permute-done.3), channel_id=1, source_target_pairs={{32,0},{64,32},{96,64},{128,96},{160,128},{192,160},{224,192},{256... | collective-permute-start | bytes 786440 | tf_op jit(solution)/shard_map/ppermute | solution.py:20
  60.8 3.1 collective-permute-done.4
  63.9 5.9 %collective-permute-start.5 = (bf16[4,1,8,2,2048]{4,3,2,1,0:T(2,128)(2,1)S(1)}, bf16[4,1,8,2,2048]{4,3,2,1,0:T(2,128)(2,1)S(1)}, u32[]{:S(2)}, u32[]{:S(2)}) collective-permute-start(bf16[4,1,8,2,2048]{4,3,2,1,0:T(2,128)(2,1)S(1)} %collective-permute-done.4), channel_id=1, source_target_pairs={{32,0},{64,32},{96,64},{128,96},{160,128},{192,160},{224,192},{256... | collective-permute-start | bytes 786440 | tf_op jit(solution)/shard_map/ppermute | solution.py:20
  70.1 3.1 collective-permute-done.5
  73.1 5.9 %collective-permute-start.6 = (bf16[4,1,8,2,2048]{4,3,2,1,0:T(2,128)(2,1)S(1)}, bf16[4,1,8,2,2048]{4,3,2,1,0:T(2,128)(2,1)S(1)}, u32[]{:S(2)}, u32[]{:S(2)}) collective-permute-start(bf16[4,1,8,2,2048]{4,3,2,1,0:T(2,128)(2,1)S(1)} %collective-permute-done.5), channel_id=1, source_target_pairs={{32,0},{64,32},{96,64},{128,96},{160,128},{192,160},{224,192},{256... | collective-permute-start | bytes 786440 | tf_op jit(solution)/shard_map/ppermute | solution.py:20
  79.3 3.1 collective-permute-done.6
  82.3 5.9 %collective-permute-start.7 = (bf16[4,1,8,2,2048]{4,3,2,1,0:T(2,128)(2,1)S(1)}, bf16[4,1,8,2,2048]{4,3,2,1,0:T(2,128)(2,1)S(1)}, u32[]{:S(2)}, u32[]{:S(2)}) collective-permute-start(bf16[4,1,8,2,2048]{4,3,2,1,0:T(2,128)(2,1)S(1)} %collective-permute-done.6), channel_id=1, source_target_pairs={{32,0},{64,32},{96,64},{128,96},{160,128},{192,160},{224,192},{256... | collective-permute-start | bytes 786440 | tf_op jit(solution)/shard_map/ppermute | solution.py:20
  88.5 3.2 collective-permute-done.7
  91.9 1.4 copy-done.1
  93.3 80.0 %while.10 = (s32[]{:T(128)}, f32[4,8,16384]{2,1,0:T(8,128)}, s32[4]{0:T(128)S(1)}, s32[32]{0:T(128)S(1)}, bf16[4,1,8,2,2048]{4,3,2,1,0:T(2,128)(2,1)S(1)}, /*ind...) while((s32[]{:T(128)}, f32[4,8,16384]{2,1,0:T(8,128)}, ...), condition=%wide.region_3.4_spmd, body=%wide.region_2.3_spmd.sunk | while | flops 6452021248 | bytes 56108012 | solution.py:76
  94.8 1.6 gather_fusion.1
  96.9 1.0 fusion.44
  98.3 3.3 gather_fusion
  102.1 1.0 fusion.42
  103.5 1.6 multiply_add_fusion.2
  105.7 6.7 %fusion.45 = f32[512,256]{1,0:T(8,128)S(1)} fusion(f32[4096,256]{1,0:T(8,128)S(1)} %copy-done, f32[512,2048]{1,0:T(8,128)S(1)} %bitcast.98, f32[512,2048]{1,0:T(8,128)S(1)} %bitcast.97), kind=kOutput, calls=%fused_computation.8.clone.1 | convolution fusion | flops 6444679168 | bytes 13107200 | tf_op jit(solution)/shard_map/while/body/eval_jaxpr/dot_general | solution.py:73
  114.8 1.6 gather_fusion.1
  116.9 1.0 fusion.44
  118.3 3.3 gather_fusion
  122.1 1.0 fusion.42
  123.5 1.6 multiply_add_fusion.2
  125.7 6.7 %fusion.45 = f32[512,256]{1,0:T(8,128)S(1)} fusion(f32[4096,256]{1,0:T(8,128)S(1)} %copy-done, f32[512,2048]{1,0:T(8,128)S(1)} %bitcast.98, f32[512,2048]{1,0:T(8,128)S(1)} %bitcast.97), kind=kOutput, calls=%fused_computation.8.clone.1 | convolution fusion | flops 6444679168 | bytes 13107200 | tf_op jit(solution)/shard_map/while/body/eval_jaxpr/dot_general | solution.py:73
  134.8 1.6 gather_fusion.1
  136.9 1.0 fusion.44
  138.3 3.3 gather_fusion
  142.1 1.0 fusion.42
  143.5 1.6 multiply_add_fusion.2
  145.7 6.7 %fusion.45 = f32[512,256]{1,0:T(8,128)S(1)} fusion(f32[4096,256]{1,0:T(8,128)S(1)} %copy-done, f32[512,2048]{1,0:T(8,128)S(1)} %bitcast.98, f32[512,2048]{1,0:T(8,128)S(1)} %bitcast.97), kind=kOutput, calls=%fused_computation.8.clone.1 | convolution fusion | flops 6444679168 | bytes 13107200 | tf_op jit(solution)/shard_map/while/body/eval_jaxpr/dot_general | solution.py:73
  154.8 1.6 gather_fusion.1
  156.9 1.0 fusion.44
  158.3 3.3 gather_fusion
  162.1 1.0 fusion.42
  163.5 1.6 multiply_add_fusion.2
  165.7 6.7 %fusion.45 = f32[512,256]{1,0:T(8,128)S(1)} fusion(f32[4096,256]{1,0:T(8,128)S(1)} %copy-done, f32[512,2048]{1,0:T(8,128)S(1)} %bitcast.98, f32[512,2048]{1,0:T(8,128)S(1)} %bitcast.97), kind=kOutput, calls=%fused_computation.8.clone.1 | convolution fusion | flops 6444679168 | bytes 13107200 | tf_op jit(solution)/shard_map/while/body/eval_jaxpr/dot_general | solution.py:73
  172.5 0.9 constant_dynamic-update-slice_fusion.3
  173.6 304.9 %all-reduce.2.cloned.1.call-done = f32[32,16384]{1,0:T(8,128)} async-done(((f32[32,16384]{1,0:T(8,128)}), f32[32,16384]{1,0:T(8,128)}) %all-reduce.2.cloned.1.call-update) | async-done | bytes 2097168 | tf_op jit(solution)/shard_map/psum | solution.py:83
  478.5 2.4 fusion.20
  (81 shorter events, 18.1 us)
Async XLA Ops:
  6.5 471.9 %all-reduce.2.cloned.1.call-start = ((), (), s32[]{:S(2)}) async-start(), calls=%async_computation | async-start | bytes 4194304 | tf_op jit(solution)/shard_map/psum | solution.py:83
  9.1 19.2 %collective-permute-start = (bf16[4,1,8,2,2048]{4,3,2,1,0:T(2,128)(2,1)S(1)}, bf16[4,1,8,2,2048]{4,3,2,1,0:T(2,128)(2,1)S(1)}, u32[]{:S(2)}, u32[]{:S(2)}) collective-permute-start(bf16[4,1,8,2,2048]{4,3,2,1,0:T(2,128)(2,1)S(1)} %bitcast.107), channel_id=1, source_target_pairs={{32,0},{64,32},{96,64},{128,96},{160,128},{192,160},{224,192},{256... | collective-permute-start | bytes 786440 | tf_op jit(solution)/shard_map/ppermute | solution.py:20
  25.8 2.3 copy-start.2
  28.3 8.6 %collective-permute-start.1 = (bf16[4,1,8,2,2048]{4,3,2,1,0:T(2,128)(2,1)S(1)}, bf16[4,1,8,2,2048]{4,3,2,1,0:T(2,128)(2,1)S(1)}, u32[]{:S(2)}, u32[]{:S(2)}) collective-permute-start(bf16[4,1,8,2,2048]{4,3,2,1,0:T(2,128)(2,1)S(1)} %collective-permute-done), channel_id=1, source_target_pairs={{32,0},{64,32},{96,64},{128,96},{160,128},{192,160},{224,192},{256... | collective-permute-start | bytes 786440 | tf_op jit(solution)/shard_map/ppermute | solution.py:20
  36.9 8.2 %collective-permute-start.2 = (bf16[4,1,8,2,2048]{4,3,2,1,0:T(2,128)(2,1)S(1)}, bf16[4,1,8,2,2048]{4,3,2,1,0:T(2,128)(2,1)S(1)}, u32[]{:S(2)}, u32[]{:S(2)}) collective-permute-start(bf16[4,1,8,2,2048]{4,3,2,1,0:T(2,128)(2,1)S(1)} %collective-permute-done.1), channel_id=1, source_target_pairs={{32,0},{64,32},{96,64},{128,96},{160,128},{192,160},{224,192},{256... | collective-permute-start | bytes 786440 | tf_op jit(solution)/shard_map/ppermute | solution.py:20
  45.2 9.5 %collective-permute-start.3 = (bf16[4,1,8,2,2048]{4,3,2,1,0:T(2,128)(2,1)S(1)}, bf16[4,1,8,2,2048]{4,3,2,1,0:T(2,128)(2,1)S(1)}, u32[]{:S(2)}, u32[]{:S(2)}) collective-permute-start(bf16[4,1,8,2,2048]{4,3,2,1,0:T(2,128)(2,1)S(1)} %collective-permute-done.2), channel_id=1, source_target_pairs={{32,0},{64,32},{96,64},{128,96},{160,128},{192,160},{224,192},{256... | collective-permute-start | bytes 786440 | tf_op jit(solution)/shard_map/ppermute | solution.py:20
  54.7 9.2 %collective-permute-start.4 = (bf16[4,1,8,2,2048]{4,3,2,1,0:T(2,128)(2,1)S(1)}, bf16[4,1,8,2,2048]{4,3,2,1,0:T(2,128)(2,1)S(1)}, u32[]{:S(2)}, u32[]{:S(2)}) collective-permute-start(bf16[4,1,8,2,2048]{4,3,2,1,0:T(2,128)(2,1)S(1)} %collective-permute-done.3), channel_id=1, source_target_pairs={{32,0},{64,32},{96,64},{128,96},{160,128},{192,160},{224,192},{256... | collective-permute-start | bytes 786440 | tf_op jit(solution)/shard_map/ppermute | solution.py:20
  63.9 9.2 %collective-permute-start.5 = (bf16[4,1,8,2,2048]{4,3,2,1,0:T(2,128)(2,1)S(1)}, bf16[4,1,8,2,2048]{4,3,2,1,0:T(2,128)(2,1)S(1)}, u32[]{:S(2)}, u32[]{:S(2)}) collective-permute-start(bf16[4,1,8,2,2048]{4,3,2,1,0:T(2,128)(2,1)S(1)} %collective-permute-done.4), channel_id=1, source_target_pairs={{32,0},{64,32},{96,64},{128,96},{160,128},{192,160},{224,192},{256... | collective-permute-start | bytes 786440 | tf_op jit(solution)/shard_map/ppermute | solution.py:20
  73.1 9.2 %collective-permute-start.6 = (bf16[4,1,8,2,2048]{4,3,2,1,0:T(2,128)(2,1)S(1)}, bf16[4,1,8,2,2048]{4,3,2,1,0:T(2,128)(2,1)S(1)}, u32[]{:S(2)}, u32[]{:S(2)}) collective-permute-start(bf16[4,1,8,2,2048]{4,3,2,1,0:T(2,128)(2,1)S(1)} %collective-permute-done.5), channel_id=1, source_target_pairs={{32,0},{64,32},{96,64},{128,96},{160,128},{192,160},{224,192},{256... | collective-permute-start | bytes 786440 | tf_op jit(solution)/shard_map/ppermute | solution.py:20
  82.3 9.3 %collective-permute-start.7 = (bf16[4,1,8,2,2048]{4,3,2,1,0:T(2,128)(2,1)S(1)}, bf16[4,1,8,2,2048]{4,3,2,1,0:T(2,128)(2,1)S(1)}, u32[]{:S(2)}, u32[]{:S(2)}) collective-permute-start(bf16[4,1,8,2,2048]{4,3,2,1,0:T(2,128)(2,1)S(1)} %collective-permute-done.6), channel_id=1, source_target_pairs={{32,0},{64,32},{96,64},{128,96},{160,128},{192,160},{224,192},{256... | collective-permute-start | bytes 786440 | tf_op jit(solution)/shard_map/ppermute | solution.py:20
  91.9 1.4 copy-start.1
  93.3 80.1 %copy-start.3 = (s32[1,32]{1,0:T(1,128)S(1)}, s32[1,32]{1,0:T(1,128)}, u32[]{:S(2)}) copy-start(s32[1,32]{1,0:T(1,128)} %param.9) | copy-start | bytes 388
  103.5 2.2 copy-start
  123.5 2.2 copy-start
  143.5 2.2 copy-start
  163.5 2.2 copy-start
Sparse Core Ops, SparseCore 0:
  173.5 304.9 all-reduce.1
where the time goes:
time: 489 us; the launch traced here: 488 us
  waiting for transfers between devices  330 us (67%)
  starting transfers between devices  43.8 us (9%)
  local copies, waits for them, and re-layouts  43 us (9%)
  matrix products  29.2 us (6%)
  other arithmetic  24.5 us (5%)
  between operations  14.3 us (3%)
    psum x1, waiting for transfers between devices, local(): totals = lax.psum(flat_stack, 'tm')  305 us
    ppermute x8, starting transfers between devices, shifted(): return lax.ppermute(block, axis, route)  43.8 us
    dot_general x4, matrix products, block_group(): jnp.dot(joined, joint_table, precision=high, preferred_element_type=jnp.f...  26.8 us
    ppermute x8, waiting for transfers between devices, shifted(): return lax.ppermute(block, axis, route)  25.6 us
    gather x4, local copies, waits for them, and re-layouts, block_group(): far_side = jnp.take(arrived, far_rows, axis=0).astype(jnp.float32)  13.1 us
  transfers between devices with their start and end apart: 9, of which 8 were waited for; matrix products, arithmetic and copies ran while one was open for 3% of the time, Pallas kernels for 0%

commit v1 on v0

v1 whole, which is shorter than its diff:
```python
import functools
import math

import jax
import jax.numpy as jnp
import numpy as np
from jax import lax
from jax.experimental import pallas as pl
from jax.experimental.pallas import tpu as pltpu
from jax.sharding import PartitionSpec as P

CB = 8
G = 4
CG = G * CB
LAGS = 256
SLOTS = 2
EPS = 1e-05
GROUPS = 16
WIN = 32
F = 2048
JJ = 4
PHI = F // JJ
MESSAGE = JJ * 2 * CG

BF16 = jnp.bfloat16
F32 = jnp.float32


def params():
    return pltpu.CompilerParams(vmem_limit_bytes=40 << 20)


def whiten_kernel(x_ref, valid_ref, out_ref):
    raw = x_ref[...].astype(F32)
    squares = jnp.sum(raw * raw, axis=(0, 2), keepdims=True)
    mean_power = squares * (1.0 / (2 * F))
    white = (raw * lax.rsqrt(mean_power + EPS)).astype(BF16).astype(F32)
    white = white * valid_ref[0].astype(F32)
    white = white.reshape(2 * CG, F)
    for pair in range(JJ // 2):
        rows = jnp.concatenate(
            [white[:, (2 * pair + j) * PHI : (2 * pair + j + 1) * PHI] for j in range(2)], axis=0
        )
        out_ref[:, pair * 128 : (pair + 1) * 128] = rows.T.astype(BF16)


def whiten(spectra, valid):
    return pl.pallas_call(
        whiten_kernel,
        out_shape=jax.ShapeDtypeStruct((PHI, MESSAGE), BF16),
        in_specs=[
            pl.BlockSpec(memory_space=pltpu.VMEM),
            pl.BlockSpec(memory_space=pltpu.SMEM),
        ],
        out_specs=pl.BlockSpec(memory_space=pltpu.VMEM),
        compiler_params=params(),
    )(spectra, valid)


def near_tables():
    far_re = np.zeros((MESSAGE, 256), np.float32)
    far_im = np.zeros((MESSAGE, 256), np.float32)
    for r in range(G):
        for j in range(JJ):
            for i in range(CB):
                re_row = (j * 2) * CG + r * CB + i
                im_row = re_row + CG
                re_lane = r * 64 + (j * 2) * CB + i
                im_lane = re_lane + CB
                far_re[re_row, re_lane] = 1
                far_re[im_row, im_lane] = 1
                far_im[im_row, re_lane] = 1
                far_im[re_row, im_lane] = -1
    return far_re, far_im


def cross_kernel(r_ref, slots_ref, near_re_ref, near_im_ref, out_ref, far_ref, near_ref):
    quarter = lax.broadcasted_iota(jnp.int32, (32, 128), 1) // 32
    for g4 in range(GROUPS // 4):
        for q4 in range(2):
            block = r_ref[g4 * 128 : (g4 + 1) * 128, q4 * 128 : (q4 + 1) * 128].astype(F32)
            turned = block.T
            for g in range(4):
                rows = None
                for q in range(4):
                    piece = turned[q * 32 : (q + 1) * 32, :]
                    shift = ((q - g) * 32) % 128
                    if shift:
                        piece = pltpu.roll(piece, shift, 1)
                    rows = piece if rows is None else jnp.where(quarter == q, piece, rows)
                start = (g4 * 4 + g) * 32
                far_ref[start : start + 32, q4 * 128 : (q4 + 1) * 128] = rows.astype(BF16)
    lane_j = lax.broadcasted_iota(jnp.int32, (32, 256), 1) // 16 % JJ
    for part, table in enumerate((near_re_ref, near_im_ref)):
        spread = jnp.dot(r_ref[...], table[...], preferred_element_type=F32)
        for g in range(GROUPS):
            rows = spread[g * 32 : (g + 1) * 32]
            for j in range(JJ):
                start = (j * 2 + part) * 32
                near_ref[g, start : start + 32, :] = jnp.where(lane_j == j, rows, 0.0).astype(BF16)

    lanes = lax.broadcasted_iota(jnp.int32, (512, 512), 1)
    first_half = lax.broadcasted_iota(jnp.int32, (256, 128), 1) < 64

    def one_group(g, _):
        slots = pltpu.roll(slots_ref[...], jnp.where(g == 0, 0, 128 - g), 1)
        slot = slots[:, 0:1]
        far_row = slot >> 2
        near_blk = slot & 3
        pick = jnp.where(lanes == far_row, 1.0, 0.0).astype(BF16)
        far = jnp.dot(pick, far_ref[...], preferred_element_type=F32).astype(BF16)
        cross = jnp.dot(far, near_ref[g], preferred_element_type=F32)
        half = jnp.where(near_blk >= 2, cross[:, 128:], cross[:, :128])
        turned = pltpu.roll(half, 64, 1)
        odd = (near_blk & 1) == 1
        low = jnp.where(odd, turned, half)[:256]
        high = jnp.where(odd, half, turned)[256:]
        start = pl.multiple_of(g * 256, 256)
        out_ref[pl.ds(start, 256), :] = jnp.where(first_half, low, high).astype(BF16)
        return 0

    lax.fori_loop(0, GROUPS, one_group, 0)


def cross(received, slots):
    near_re, near_im = (jnp.asarray(t, BF16) for t in near_tables())
    return pl.pallas_call(
        cross_kernel,
        out_shape=jax.ShapeDtypeStruct((GROUPS * 32 * CB, 128), BF16),
        in_specs=[pl.BlockSpec(memory_space=pltpu.VMEM)] * 4,
        out_specs=pl.BlockSpec(memory_space=pltpu.VMEM),
        scratch_shapes=[
            pltpu.VMEM((512, 256), BF16),
            pltpu.VMEM((GROUPS, 256, 256), BF16),
        ],
        compiler_params=params(),
    )(received, slots, near_re, near_im)


def lag_tables():
    shifts = np.arange(LAGS) - LAGS // 2
    angle = np.pi / F * (np.arange(PHI)[:, None] * shifts[None, :] % (2 * F))
    base = np.concatenate([np.cos(angle), np.sin(angle)], axis=1)
    high = base.astype(jnp.bfloat16)
    low = (base - high.astype(np.float64)).astype(jnp.bfloat16)
    turn = np.pi / F * (PHI * np.arange(JJ)[:, None] * shifts[None, :] % (2 * F))
    cos, sin = np.cos(turn), np.sin(turn)
    mix = np.stack([np.stack([cos, -sin], 1), np.stack([-sin, -cos], 1)], 1)
    mix = mix.reshape(JJ * 2 * 2, LAGS) / math.sqrt(F * WIN)
    return high, low, mix.astype(np.float32)


def lag_kernel(m_ref, high_ref, low_ref, mix_ref, out_ref, wide_ref, turned_ref):
    wide_ref[...] = m_ref[...].astype(F32)
    for far in range(CB):
        rows = wide_ref[pl.ds(far, PHI, stride=CB), :]
        turned_ref[far * 128 : (far + 1) * 128, :] = rows.T.astype(BF16)
    sums = jnp.dot(turned_ref[...], high_ref[...], preferred_element_type=F32)
    sums = sums + jnp.dot(turned_ref[...], low_ref[...], preferred_element_type=F32)
    for far in range(CB):
        for slot in range(SLOTS):
            total = None
            for q in range(JJ * 2):
                start = far * 128 + slot * 64 + q * CB
                rows = sums[start : start + CB]
                term = rows[:, :LAGS] * mix_ref[2 * q : 2 * q + 1, :]
                term = term + rows[:, LAGS:] * mix_ref[2 * q + 1 : 2 * q + 2, :]
                total = term if total is None else total + term
            out_ref[slot, :, far * LAGS : (far + 1) * LAGS] = total


def lags(arrived):
    high, low, mix = lag_tables()
    return pl.pallas_call(
        lag_kernel,
        out_shape=jax.ShapeDtypeStruct((SLOTS, CB, CB * LAGS), F32),
        in_specs=[pl.BlockSpec(memory_space=pltpu.VMEM)] * 4,
        out_specs=pl.BlockSpec(memory_space=pltpu.VMEM),
        scratch_shapes=[
            pltpu.VMEM((PHI * CB, 128), F32),
            pltpu.VMEM((CB * 128, PHI), BF16),
        ],
        compiler_params=params(),
    )(arrived, jnp.asarray(high), jnp.asarray(low), jnp.asarray(mix))


def slot_rows(pair_code, block_owner):
    codes = pair_code[0]
    owners = block_owner[0]
    blocks = codes.shape[0]
    order = jnp.arange(blocks, dtype=jnp.int32)
    earlier = order[None, :] < order[:, None]
    rank = jnp.sum((earlier & (owners[None, :] == owners[:, None])).astype(jnp.int32), axis=1)
    spot = rank * 32 + owners
    filled = spot[None, :] == jnp.arange(SLOTS * 32, dtype=jnp.int32)[:, None]
    mine = jnp.max(jnp.where(filled, codes[None, :] + 1, 0), axis=1)
    group = lax.axis_index("chan")
    groups = jnp.arange(GROUPS, dtype=jnp.int32)
    placed = jnp.where(groups[:, None] == group, mine[None, :], 0).astype(F32)
    table = lax.psum(placed, "chan").astype(jnp.int32).T
    code = table - 1
    near_blk = code // 36
    dist = code // 4 % 9
    far_blk = code % 4
    far_row = (groups[None, :] + dist) % GROUPS * CG + far_blk * CB
    base = far_row * 4 + near_blk
    inner = jnp.arange(CB, dtype=jnp.int32)[None, :, None] * 4
    rows = jnp.where(table[:, None, :] > 0, base[:, None, :] + inner, -1)
    rows = rows.reshape(SLOTS * 32 * CB, GROUPS)
    return jnp.pad(rows, ((0, 0), (0, 128 - GROUPS)))


def local(spectra, window_valid, pair_code, block_owner):
    both = ("chan", "tm")
    slots = slot_rows(pair_code, block_owner)
    parts_first = spectra[0].transpose(1, 0, 2)
    sent = whiten(parts_first, window_valid).reshape(PHI, 2, 128)
    received = lax.all_to_all(sent, both, 0, 0, tiled=True).reshape(GROUPS * WIN, MESSAGE)
    crossed = cross(received, slots).reshape(GROUPS * 32, CB, 128)
    arrived = lax.all_to_all(crossed, both, 0, 0, tiled=True).reshape(PHI * CB, 128)
    return lags(arrived)[None]


def solution(mesh):
    return jax.shard_map(
        local,
        mesh=mesh,
        in_specs=(P("tm", "chan", None, None), P("tm"), P("chan", None), P("chan", None)),
        out_specs=P("chan", "tm", None, None),
        check_vma=False,
    )
```

time: 489 us -> 154 us (0.31)
  waiting for transfers between devices: 330 us -> 0.01 us
  blocking collectives: 0 us -> 113 us
  local copies, waits for them, and re-layouts: 43 us -> 4 us
  matrix products: 29.2 us -> 0 us
  other arithmetic: 24.5 us -> 0.6 us
  starting transfers between devices: 43.8 us -> 22.2 us
  between operations: 14.3 us -> 0.79 us
  Pallas kernels: 0 us -> 13.5 us
    psum x1 -> x0, waiting for transfers between devices: 305 us -> none  [local(): totals = lax.psum(flat_stack, 'tm')]
    all_to_all x0 -> x1, blocking collectives: none -> 62.1 us  [local(): lax.all_to_all(crossed, both, 0, 0, tiled=True).reshape(PHI * CB, 128)]
    psum x0 -> x1, blocking collectives: none -> 50.9 us  [slot_rows(): table = lax.psum(placed, 'chan').astype(jnp.int32).T]
    ppermute x8 -> x0, starting transfers between devices: 43.8 us -> none  [shifted(): return lax.ppermute(block, axis, route)]
    dot_general x5 -> x0, matrix products: 29.2 us -> none  [the longest x4 26.8 us: block_group(): jnp.dot(joined, joint_table, precision=high, preferred_element_type=jnp.f...]
    ppermute x8 -> x0, waiting for transfers between devices: 25.6 us -> none  [shifted(): return lax.ppermute(block, axis, route)]
    all_to_all x0 -> x1, starting transfers between devices: none -> 22.2 us  [local(): lax.all_to_all(sent, both, 0, 0, tiled=True).reshape(GROUPS * WIN, MESSAGE)]
    gather x8 -> x0, local copies, waits for them, and re-layouts: 19.5 us -> none  [the longest x4 13.1 us: block_group(): far_side = jnp.take(arrived, far_rows, axis=0).astype(jnp.float32)]
  transfers between devices with their start and end apart: 9 -> 1, of which waited for: 8 -> 0; matrix products, arithmetic and copies ran while one was open for 3% -> 0% of each run, Pallas kernels for 0% -> 0%
where the time goes in v1:
time: 154 us
  blocking collectives  113 us (73%)
  starting transfers between devices  22.2 us (14%)
  Pallas kernels  13.5 us (9%)
  local copies, waits for them, and re-layouts  4 us (3%)
    all_to_all x1, blocking collectives, local(): lax.all_to_all(crossed, both, 0, 0, tiled=True).reshape(PHI * CB, 128)  62.1 us
    psum x1, blocking collectives, slot_rows(): table = lax.psum(placed, 'chan').astype(jnp.int32).T  50.9 us
    all_to_all x1, starting transfers between devices, local(): lax.all_to_all(sent, both, 0, 0, tiled=True).reshape(GROUPS * WIN, MESSAGE)  22.2 us
    pallas_call x1, Pallas kernels, cross(): pl.pallas_call(cross_kernel, out_shape=jax.ShapeDtypeStruct((GROUPS * 32...  11.1 us
    unnamed x16, local copies, waits for them, and re-layouts  3.13 us
  transfers between devices with their start and end apart: 1, of which 0 were waited for; matrix products, arithmetic and copies ran while one was open for 0% of the time, Pallas kernels for 0%

profile of v1, /device:TPU:1, one launch (start us, length us, event | category | flops | bytes accessed | tf_op | source)
XLA Modules:
  0.0 154.1 jit_solution(16539062734910192721)
XLA Ops:
  0.7 1.0 copy.17
  1.7 0.3 shard_map.91
  2.0 0.8 reshape.40
  2.7 22.2 %all-to-all-start = ((bf16[512,2,128]{2,1,0:T(2,128)(2,1)}), bf16[512,2,128]{2,1,0:T(2,128)(2,1)S(1)}, u32[]{:S(2)}, u32[]{:S(2)}) async-start(bf16[512,2,128]{2,1,0:T(2,128)(2,1)} %reshape.40), calls=%async_computation | async-start | bytes 524288 | tf_op jit(solution)/shard_map/all_to_all | solution.py:218
  24.9 0.0 copy-start.5
  24.9 0.6 copy-done.5
  25.6 0.0 copy-start.6
  25.6 0.2 convert_reduce_fusion
  25.8 0.5 copy-done.6
  26.2 0.1 select_reduce_fusion
  26.3 0.1 select_convert_fusion
  26.4 50.9 %psum.7 = f32[16,64]{0,1:T(8,128)S(1)} all-reduce(f32[16,64]{0,1:T(8,128)S(1)} %select_convert_fusion), channel_id=1, replica_groups=mesh['chan'=16,'tm'=32] {'chan'}, use_global_device_ids=true, to_apply=%region_2.3 | all-reduce | flops 1024 | bytes 8192 | tf_op jit(solution)/shard_map/psum | solution.py:200
  77.4 0.1 add.79
  77.5 0.1 fusion.7
  77.6 0.1 fusion
  77.7 0.0 all-to-all-done
  77.8 0.0 copy-start.2
  77.8 0.0 copy-start.3
  77.8 0.8 copy-done.2
  78.7 0.1 copy-done.3
  78.7 11.1 %shard_map.92 = bf16[4096,128]{1,0:T(8,128)(2,1)S(1)} custom-call(bf16[512,256]{1,0:T(8,128)(2,1)S(1)} %bitcast.55, s32[512,128]{1,0:T(8,128)S(1)} %pad.4.slots_ref, bf16[256,256]{1,0:T(8,128)(2,1)S(1)} %copy-done.3, bf16[256,256]{1,0:T(8,128)(2,1)S(1)} %copy-done.2), custom_call_target="tpu_custom_call" | custom-call | tf_op jit(solution)/shard_map/pallas_call | solution.py:127
  89.8 0.0 copy-start
  89.8 0.0 copy-start.1
  89.8 0.0 copy-start.4
  89.9 62.1 %all_to_all.10 = bf16[512,8,128]{2,1,0:T(8,128)(2,1)S(1)} all-to-all(bf16[512,8,128]{2,1,0:T(8,128)(2,1)S(1)} %bitcast.53), channel_id=1, replica_groups=mesh['chan'=16,'tm'=32] {'chan','tm'}, dimensions={0} | all-to-all | bytes 2097152 | tf_op jit(solution)/shard_map/all_to_all | solution.py:220
  152.0 0.0 copy-done
  152.0 0.0 copy-done.1
  152.0 0.0 copy-done.4
  152.0 2.1 %shard_map.93 = f32[2,8,2048]{2,1,0:T(8,128)} custom-call(bf16[4096,128]{1,0:T(8,128)(2,1)S(1)} %bitcast.54, bf16[512,512]{1,0:T(8,128)(2,1)S(1)} %copy-done.1, bf16[512,512]{1,0:T(8,128)(2,1)S(1)} %copy-done, f32[16,256]{1,0:T(8,128)S(1)} %copy-done.4), custom_call_target="tpu_custom_call" | custom-call | tf_op jit(solution)/shard_map/pallas_call | solution.py:174
  (7 shorter events, 0.1 us)
Async XLA Ops:
  2.7 75.0 %all-to-all-start = ((bf16[512,2,128]{2,1,0:T(2,128)(2,1)}), bf16[512,2,128]{2,1,0:T(2,128)(2,1)S(1)}, u32[]{:S(2)}, u32[]{:S(2)}) async-start(bf16[512,2,128]{2,1,0:T(2,128)(2,1)} %reshape.40), calls=%async_computation | async-start | bytes 524288 | tf_op jit(solution)/shard_map/all_to_all | solution.py:218
  24.9 0.7 copy-start.5
  25.6 0.7 copy-start.6
  77.8 0.9 copy-start.2
  77.8 1.0 copy-start.3
  89.8 62.1 %copy-start = (bf16[512,512]{1,0:T(8,128)(2,1)S(1)}, bf16[512,512]{1,0:T(8,128)(2,1)}, u32[]{:S(2)}) copy-start(bf16[512,512]{1,0:T(8,128)(2,1)} %constant.87.clone.low_ref) | copy-start | bytes 1572868
  89.8 62.1 %copy-start.1 = (bf16[512,512]{1,0:T(8,128)(2,1)S(1)}, bf16[512,512]{1,0:T(8,128)(2,1)}, u32[]{:S(2)}) copy-start(bf16[512,512]{1,0:T(8,128)(2,1)} %constant.86.clone.high_ref) | copy-start | bytes 1572868
  89.8 62.1 %copy-start.4 = (f32[16,256]{1,0:T(8,128)S(1)}, f32[16,256]{1,0:T(8,128)}, u32[]{:S(2)}) copy-start(f32[16,256]{1,0:T(8,128)} %constant.88.clone.mix_ref) | copy-start | bytes 49156

commit v2 on v1

v2 whole, which is shorter than its diff:
```python
import math

import jax
import jax.numpy as jnp
import numpy as np
from jax import lax
from jax.experimental import pallas as pl
from jax.experimental.pallas import tpu as pltpu
from jax.sharding import PartitionSpec as P

CB = 8
G = 4
CG = G * CB
LAGS = 256
SLOTS = 2
EPS = 1e-05
GROUPS = 16
WIN = 32
BLOCKS = 32
F = 2048
JJ = 4
PHI = F // JJ
MESSAGE = JJ * 2 * CG
ROWS = 4

BF16 = jnp.bfloat16
F32 = jnp.float32


def params():
    return pltpu.CompilerParams(vmem_limit_bytes=40 << 20)


def whiten_kernel(x_ref, valid_ref, code_ref, owner_ref, out_ref, wide_ref, sent_ref):
    wide_ref[...] = x_ref[...].astype(F32)
    tiles = F // 128
    raw = [
        [wide_ref[pl.ds(tile * 2 + part, CG, stride=tiles * 2), :] for tile in range(tiles)]
        for part in range(2)
    ]
    squares = sum(block * block for side in raw for block in side)
    mean_power = jnp.sum(squares, axis=1, keepdims=True) * (1.0 / (2 * F))
    scale = lax.rsqrt(mean_power + EPS)
    valid = valid_ref[0].astype(F32)
    for pair in range(JJ // 2):
        for tile in range(PHI // 128):
            rows = jnp.concatenate(
                [
                    (raw[part][j * (PHI // 128) + tile] * scale).astype(BF16).astype(F32) * valid
                    for j in (2 * pair, 2 * pair + 1)
                    for part in range(2)
                ],
                axis=0,
            )
            sent_ref[pl.ds(tile * 128 * ROWS + pair, 128, stride=ROWS), :] = rows.T
    code = code_ref[...]
    owner = owner_ref[...]
    near_blk = code // 36
    lane = lax.broadcasted_iota(jnp.int32, (1, 128), 1)
    lone = jnp.concatenate([owner, jnp.full((1, 128 - BLOCKS), -1, jnp.int32)], axis=1)
    rank = jnp.zeros((1, 128), jnp.int32)
    for back in range(1, BLOCKS):
        same = pltpu.roll(lone, back, 1) == lone
        rank = rank + jnp.where(same & (lane >= back), 1, 0)
    fields = jnp.concatenate([code - near_blk * 36, near_blk, owner, rank[:, :BLOCKS]], axis=1)
    fields = jnp.broadcast_to(fields.astype(F32), (PHI, 128))
    sent_ref[pl.ds(2, PHI, stride=ROWS), :] = fields
    sent_ref[pl.ds(3, PHI, stride=ROWS), :] = fields
    out_ref[...] = sent_ref[...].astype(BF16)


def whiten(spectra, valid, codes, owners):
    vmem = pl.BlockSpec(memory_space=pltpu.VMEM)
    return pl.pallas_call(
        whiten_kernel,
        out_shape=jax.ShapeDtypeStruct((PHI * ROWS, 128), BF16),
        in_specs=[vmem, pl.BlockSpec(memory_space=pltpu.SMEM), vmem, vmem],
        out_specs=vmem,
        scratch_shapes=[
            pltpu.VMEM((CG * F // 64, 128), F32),
            pltpu.VMEM((PHI * ROWS, 128), F32),
        ],
        compiler_params=params(),
    )(spectra, valid, codes, owners)


def near_tables():
    far_re = np.zeros((MESSAGE, 256), np.float32)
    far_im = np.zeros((MESSAGE, 256), np.float32)
    for r in range(G):
        for j in range(JJ):
            for i in range(CB):
                re_row = (j * 2) * CG + r * CB + i
                im_row = re_row + CG
                re_lane = r * 64 + (j * 2) * CB + i
                im_lane = re_lane + CB
                far_re[re_row, re_lane] = 1
                far_re[im_row, im_lane] = 1
                far_im[im_row, re_lane] = 1
                far_im[re_row, im_lane] = -1
    return far_re, far_im


def cross_kernel(
    r_ref,
    blocks_ref,
    near_re_ref,
    near_im_ref,
    out_ref,
    wide_ref,
    own_ref,
    far_ref,
    near_ref,
    slots_ref,
):
    slots_ref[...] = jnp.zeros_like(slots_ref)
    wide_ref[...] = r_ref[...].astype(F32)
    quarter = lax.broadcasted_iota(jnp.int32, (32, 128), 1) // 32
    for g4 in range(GROUPS // 4):
        for q4 in range(2):
            block = wide_ref[pl.ds(g4 * 128 * ROWS + q4, 128, stride=ROWS), :]
            own_ref[g4 * 128 : (g4 + 1) * 128, q4 * 128 : (q4 + 1) * 128] = block.astype(BF16)
            turned = block.T
            for g in range(4):
                rows = None
                for q in range(4):
                    piece = turned[q * 32 : (q + 1) * 32, :]
                    shift = ((q - g) * 32) % 128
                    if shift:
                        piece = pltpu.roll(piece, shift, 1)
                    rows = piece if rows is None else jnp.where(quarter == q, piece, rows)
                start = (g4 * 4 + g) * 32
                far_ref[start : start + 32, q4 * 128 : (q4 + 1) * 128] = rows
    lane_j = lax.broadcasted_iota(jnp.int32, (32, 256), 1) // 16 % JJ
    for part, table in enumerate((near_re_ref, near_im_ref)):
        spread = jnp.dot(own_ref[...], table[...], preferred_element_type=F32)
        for g in range(GROUPS):
            rows = spread[g * 32 : (g + 1) * 32]
            for j in range(JJ):
                start = (j * 2 + part) * 32
                near_ref[g, start : start + 32, :] = jnp.where(lane_j == j, rows, 0.0).astype(BF16)

    def one_group(g, _):
        entries = [blocks_ref[g, k] for k in range(BLOCKS)]
        far = jnp.concatenate(
            [
                far_ref[pl.ds(pl.multiple_of(((g * G + (e >> 8)) & 63) * CB, CB), CB), :]
                for e in entries
            ],
            axis=0,
        ).astype(BF16)
        cross = jnp.dot(far, near_ref[g], preferred_element_type=F32)
        for k, e in enumerate(entries):
            near_blk, owner, slot = (e >> 6) & 3, (e >> 1) & 31, e & 1
            rows = cross[k * CB : (k + 1) * CB]
            half = jnp.where(near_blk >= 2, rows[:, 128:], rows[:, :128])
            half = jnp.where((near_blk & 1) != slot, pltpu.roll(half, 64, 1), half)
            start = pl.multiple_of((g * 32 + owner) * CB, CB)
            slots_ref[slot, pl.ds(start, CB), :] = half
        return 0

    lax.fori_loop(0, GROUPS, one_group, 0)
    first_half = lax.broadcasted_iota(jnp.int32, (256, 128), 1) < 64

    def finish(g, _):
        rows = pl.ds(pl.multiple_of(g * 256, 256), 256)
        both = jnp.where(first_half, slots_ref[0, rows, :], slots_ref[1, rows, :])
        out_ref[rows, :] = both.astype(BF16)
        return 0

    lax.fori_loop(0, GROUPS, finish, 0)


def cross(received, blocks):
    near_re, near_im = (jnp.asarray(t, BF16) for t in near_tables())
    vmem = pl.BlockSpec(memory_space=pltpu.VMEM)
    return pl.pallas_call(
        cross_kernel,
        out_shape=jax.ShapeDtypeStruct((GROUPS * 32 * CB, 128), BF16),
        in_specs=[vmem, pl.BlockSpec(memory_space=pltpu.SMEM), vmem, vmem],
        out_specs=vmem,
        scratch_shapes=[
            pltpu.VMEM((GROUPS * WIN * ROWS, 128), F32),
            pltpu.VMEM((512, 256), BF16),
            pltpu.VMEM((512, 256), F32),
            pltpu.VMEM((GROUPS, 256, 256), BF16),
            pltpu.VMEM((SLOTS, GROUPS * 32 * CB, 128), F32),
        ],
        compiler_params=params(),
    )(received, blocks, near_re, near_im)


def lag_tables():
    shifts = np.arange(LAGS) - LAGS // 2
    angle = np.pi / F * (np.arange(PHI)[:, None] * shifts[None, :] % (2 * F))
    base = np.concatenate([np.cos(angle), np.sin(angle)], axis=1)
    high = base.astype(jnp.bfloat16)
    low = (base - high.astype(np.float64)).astype(jnp.bfloat16)
    turn = np.pi / F * (PHI * np.arange(JJ)[:, None] * shifts[None, :] % (2 * F))
    cos, sin = np.cos(turn), np.sin(turn)
    mix = np.stack([np.stack([cos, -sin], 1), np.stack([-sin, -cos], 1)], 1)
    mix = mix.reshape(JJ * 2 * 2, LAGS) / math.sqrt(F * WIN)
    return high, low, mix.astype(np.float32)


def lag_kernel(m_ref, high_ref, low_ref, mix_ref, out_ref, wide_ref, turned_ref):
    wide_ref[...] = m_ref[...].astype(F32)
    for far in range(CB):
        rows = wide_ref[pl.ds(far, PHI, stride=CB), :]
        turned_ref[far * 128 : (far + 1) * 128, :] = rows.T.astype(BF16)
    sums = jnp.dot(turned_ref[...], high_ref[...], preferred_element_type=F32)
    sums = sums + jnp.dot(turned_ref[...], low_ref[...], preferred_element_type=F32)
    for far in range(CB):
        for slot in range(SLOTS):
            total = None
            for q in range(JJ * 2):
                start = far * 128 + slot * 64 + q * CB
                rows = sums[start : start + CB]
                term = rows[:, :LAGS] * mix_ref[2 * q : 2 * q + 1, :]
                term = term + rows[:, LAGS:] * mix_ref[2 * q + 1 : 2 * q + 2, :]
                total = term if total is None else total + term
            out_ref[slot, :, far * LAGS : (far + 1) * LAGS] = total


def lags(arrived):
    high, low, mix = lag_tables()
    return pl.pallas_call(
        lag_kernel,
        out_shape=jax.ShapeDtypeStruct((SLOTS, CB, CB * LAGS), F32),
        in_specs=[pl.BlockSpec(memory_space=pltpu.VMEM)] * 4,
        out_specs=pl.BlockSpec(memory_space=pltpu.VMEM),
        scratch_shapes=[
            pltpu.VMEM((PHI * CB, 128), F32),
            pltpu.VMEM((CB * 128, PHI), BF16),
        ],
        compiler_params=params(),
    )(arrived, jnp.asarray(high), jnp.asarray(low), jnp.asarray(mix))


def local(spectra, window_valid, pair_code, block_owner):
    both = ("chan", "tm")
    tiled = spectra.reshape(CG, 2, F // 128, 128).transpose(0, 2, 1, 3).reshape(CG * F // 64, 128)
    sent = whiten(tiled, window_valid, pair_code, block_owner).reshape(PHI, ROWS, 128)
    received = lax.all_to_all(sent, both, 0, 0, tiled=True)
    fields = received[::WIN, 2].astype(jnp.int32)
    far, near, owner, rank = (fields[:, i * BLOCKS : (i + 1) * BLOCKS] for i in range(4))
    blocks = far * 256 + near * 64 + owner * 2 + rank
    crossed = cross(received.reshape(GROUPS * WIN * ROWS, 128), blocks)
    crossed = crossed.reshape(GROUPS * 32, CB, 128)
    arrived = lax.all_to_all(crossed, both, 0, 0, tiled=True).reshape(PHI * CB, 128)
    return lags(arrived)[None]


def solution(mesh):
    return jax.shard_map(
        local,
        mesh=mesh,
        in_specs=(P("tm", "chan", None, None), P("tm"), P("chan", None), P("chan", None)),
        out_specs=P("chan", "tm", None, None),
        check_vma=False,
    )
```

time: 154 us -> 99.3 us (0.64)
  blocking collectives: 113 us -> 87 us
  starting transfers between devices: 22.2 us -> 0 us
  Pallas kernels: 13.5 us -> 9.68 us
  local copies, waits for them, and re-layouts: 4 us -> 1.65 us
    psum x1 -> x0, blocking collectives: 50.9 us -> none  [slot_rows(): table = lax.psum(placed, 'chan').astype(jnp.int32).T]
    all_to_all x0 -> x1, blocking collectives: none -> 44.4 us  [local(): received = lax.all_to_all(sent, both, 0, 0, tiled=True)]
    all_to_all x1 -> x0, starting transfers between devices: 22.2 us -> none  [local(): lax.all_to_all(sent, both, 0, 0, tiled=True).reshape(GROUPS * WIN, MESSAGE)]
    all_to_all x1, blocking collectives: 62.1 us -> 42.5 us  [local(): lax.all_to_all(crossed, both, 0, 0, tiled=True).reshape(PHI * CB, 128)]
    pallas_call x1, Pallas kernels: 11.1 us -> 6.83 us  [cross(): pl.pallas_call(cross_kernel, out_shape=jax.ShapeDtypeStruct((GROUPS * 32...]
  transfers between devices with their start and end apart: 1 -> 0, of which waited for: 0 -> 0; matrix products, arithmetic and copies ran while one was open for 0% -> 0% of each run, Pallas kernels for 0% -> 0%
where the time goes in v2:
time: 99.3 us; the launch traced here: 99.1 us
  blocking collectives  87 us (88%)
  Pallas kernels  9.68 us (10%)
  local copies, waits for them, and re-layouts  1.65 us (2%)
    all_to_all x1, blocking collectives, local(): received = lax.all_to_all(sent, both, 0, 0, tiled=True)  44.4 us
    all_to_all x1, blocking collectives, local(): lax.all_to_all(crossed, both, 0, 0, tiled=True).reshape(PHI * CB, 128)  42.5 us
    pallas_call x1, Pallas kernels, cross(): pl.pallas_call(cross_kernel, out_shape=jax.ShapeDtypeStruct((GROUPS * 32...  6.83 us
    pallas_call x1, Pallas kernels, lags(): pl.pallas_call(lag_kernel, out_shape=jax.ShapeDtypeStruct((SLOTS, CB, CB...  2.11 us

profile of v2, /device:TPU:1, one launch (start us, length us, event | category | flops | bytes accessed | tf_op | source)
XLA Modules:
  0.0 99.1 jit_solution(18179582181651307612)
XLA Ops:
  0.7 0.0 copy-start.6
  0.7 0.0 copy-start.7
  0.7 0.6 copy-done.6
  1.3 0.0 copy-done.7
  1.3 0.0 copy-start.2
  1.3 0.9 copy-done.2
  2.3 0.7 shard_map.91
  3.0 0.0 copy-start.3
  3.0 0.0 copy-start.4
  3.0 44.4 %all_to_all.10 = bf16[512,4,128]{2,1,0:T(4,128)(2,1)S(1)} all-to-all(bf16[512,4,128]{2,1,0:T(4,128)(2,1)S(1)} %bitcast.18), channel_id=1, replica_groups=mesh['chan'=16,'tm'=32] {'chan','tm'}, dimensions={0} | all-to-all | bytes 1048576 | tf_op jit(solution)/shard_map/all_to_all | solution.py:244
  47.5 0.1 slice_add_fusion.blocks_ref
  47.6 0.0 copy-done.3
  47.6 0.0 copy-done.4
  47.6 6.8 %shard_map.92 = bf16[4096,128]{1,0:T(8,128)(2,1)S(1)} custom-call(bf16[2048,128]{1,0:T(8,128)(2,1)S(1)} %bitcast.17, s32[16,32]{1,0:T(8,128)S(1)} %slice_add_fusion.blocks_ref, bf16[256,256]{1,0:T(8,128)(2,1)S(1)} %copy-done.4, bf16[256,256]{1,0:T(8,128)(2,1)S(1)} %copy-done.3), custom_call_target="tpu_custom_call" | custom-call | tf_op jit(solution)/shard_map/pallas_call | solution.py:177
  54.4 0.0 copy-start
  54.5 0.0 copy-start.1
  54.5 0.0 copy-start.5
  54.5 42.5 %all_to_all.11 = bf16[512,8,128]{2,1,0:T(8,128)(2,1)S(1)} all-to-all(bf16[512,8,128]{2,1,0:T(8,128)(2,1)S(1)} %bitcast.15), channel_id=1, replica_groups=mesh['chan'=16,'tm'=32] {'chan','tm'}, dimensions={0} | all-to-all | bytes 2097152 | tf_op jit(solution)/shard_map/all_to_all | solution.py:250
  97.0 0.0 copy-done
  97.0 0.0 copy-done.1
  97.0 0.0 copy-done.5
  97.0 2.1 %shard_map.93 = f32[2,8,2048]{2,1,0:T(8,128)} custom-call(bf16[4096,128]{1,0:T(8,128)(2,1)S(1)} %bitcast.16, bf16[512,512]{1,0:T(8,128)(2,1)S(1)} %copy-done.1, bf16[512,512]{1,0:T(8,128)(2,1)S(1)} %copy-done, f32[16,256]{1,0:T(8,128)S(1)} %copy-done.5), custom_call_target="tpu_custom_call" | custom-call | tf_op jit(solution)/shard_map/pallas_call | solution.py:227
  (2 shorter events, 0.0 us)
Async XLA Ops:
  0.7 0.7 copy-start.6
  0.7 0.7 copy-start.7
  1.3 0.9 copy-start.2
  3.0 44.6 %copy-start.3 = (bf16[256,256]{1,0:T(8,128)(2,1)S(1)}, bf16[256,256]{1,0:T(8,128)(2,1)}, u32[]{:S(2)}) copy-start(bf16[256,256]{1,0:T(8,128)(2,1)} %constant.17.clone.near_im_ref) | copy-start | bytes 393220
  3.0 44.6 %copy-start.4 = (bf16[256,256]{1,0:T(8,128)(2,1)S(1)}, bf16[256,256]{1,0:T(8,128)(2,1)}, u32[]{:S(2)}) copy-start(bf16[256,256]{1,0:T(8,128)(2,1)} %constant.16.clone.near_re_ref) | copy-start | bytes 393220
  54.4 42.6 %copy-start = (bf16[512,512]{1,0:T(8,128)(2,1)S(1)}, bf16[512,512]{1,0:T(8,128)(2,1)}, u32[]{:S(2)}) copy-start(bf16[512,512]{1,0:T(8,128)(2,1)} %constant.19.clone.low_ref) | copy-start | bytes 1572868
  54.5 42.6 %copy-start.1 = (bf16[512,512]{1,0:T(8,128)(2,1)S(1)}, bf16[512,512]{1,0:T(8,128)(2,1)}, u32[]{:S(2)}) copy-start(bf16[512,512]{1,0:T(8,128)(2,1)} %constant.18.clone.high_ref) | copy-start | bytes 1572868
  54.5 42.5 %copy-start.5 = (f32[16,256]{1,0:T(8,128)S(1)}, f32[16,256]{1,0:T(8,128)}, u32[]{:S(2)}) copy-start(f32[16,256]{1,0:T(8,128)} %constant.20.clone.mix_ref) | copy-start | bytes 49156

commit v3 on v2

--- a/solution.py
+++ b/solution.py
@@ -31,7 +31,29 @@
     return pltpu.CompilerParams(vmem_limit_bytes=40 << 20)
 
 
+def sent_fields(code_ref, owner_ref, sent_ref):
+    lane = lax.broadcasted_iota(jnp.int32, (1, 128), 1)
+    fill = jnp.full((1, 128 - BLOCKS), -1, jnp.int32)
+    owner = jnp.concatenate([owner_ref[...], fill], axis=1)
+    code = jnp.concatenate([code_ref[...], fill], axis=1)
+    rank = jnp.zeros((1, 128), jnp.int32)
+    for back in range(1, BLOCKS):
+        same = pltpu.roll(owner, back, 1) == owner
+        rank = rank + jnp.where(same & (lane >= back), 1, 0)
+    near_blk = code // 36
+    far = code - near_blk * 36
+    form = ((near_blk >> 1) + 2 * ((near_blk & 1) ^ rank)) * BLOCKS + lane
+    place = rank * 32 + owner
+    fields = jnp.where(lane < BLOCKS, far, pltpu.roll(form, BLOCKS, 1))
+    fields = jnp.where(lane < 2 * BLOCKS, fields, pltpu.roll(place, 2 * BLOCKS, 1))
+    fields = jnp.where(lane < 3 * BLOCKS, fields, 0)
+    fields = jnp.broadcast_to(fields.astype(F32), (PHI, 128))
+    sent_ref[pl.ds(2, PHI, stride=ROWS), :] = fields
+    sent_ref[pl.ds(3, PHI, stride=ROWS), :] = fields
+
+
 def whiten_kernel(x_ref, valid_ref, code_ref, owner_ref, out_ref, wide_ref, sent_ref):
+    sent_fields(code_ref, owner_ref, sent_ref)
     wide_ref[...] = x_ref[...].astype(F32)
     tiles = F // 128
     raw = [
@@ -53,19 +75,6 @@
                 axis=0,
             )
             sent_ref[pl.ds(tile * 128 * ROWS + pair, 128, stride=ROWS), :] = rows.T
-    code = code_ref[...]
-    owner = owner_ref[...]
-    near_blk = code // 36
-    lane = lax.broadcasted_iota(jnp.int32, (1, 128), 1)
-    lone = jnp.concatenate([owner, jnp.full((1, 128 - BLOCKS), -1, jnp.int32)], axis=1)
-    rank = jnp.zeros((1, 128), jnp.int32)
-    for back in range(1, BLOCKS):
-        same = pltpu.roll(lone, back, 1) == lone
-        rank = rank + jnp.where(same & (lane >= back), 1, 0)
-    fields = jnp.concatenate([code - near_blk * 36, near_blk, owner, rank[:, :BLOCKS]], axis=1)
-    fields = jnp.broadcast_to(fields.astype(F32), (PHI, 128))
-    sent_ref[pl.ds(2, PHI, stride=ROWS), :] = fields
-    sent_ref[pl.ds(3, PHI, stride=ROWS), :] = fields
     out_ref[...] = sent_ref[...].astype(BF16)
 
 
@@ -102,16 +111,7 @@
 
 
 def cross_kernel(
-    r_ref,
-    blocks_ref,
-    near_re_ref,
-    near_im_ref,
-    out_ref,
-    wide_ref,
-    own_ref,
-    far_ref,
-    near_ref,
-    slots_ref,
+    r_ref, blocks_ref, near_re_ref, near_im_ref, out_ref, wide_ref, own_ref, far_ref, near_ref, forms_ref, slots_ref
 ):
     slots_ref[...] = jnp.zeros_like(slots_ref)
     wide_ref[...] = r_ref[...].astype(F32)
@@ -131,44 +131,34 @@
                     rows = piece if rows is None else jnp.where(quarter == q, piece, rows)
                 start = (g4 * 4 + g) * 32
                 far_ref[start : start + 32, q4 * 128 : (q4 + 1) * 128] = rows
-    lane_j = lax.broadcasted_iota(jnp.int32, (32, 256), 1) // 16 % JJ
     for part, table in enumerate((near_re_ref, near_im_ref)):
         spread = jnp.dot(own_ref[...], table[...], preferred_element_type=F32)
-        for g in range(GROUPS):
-            rows = spread[g * 32 : (g + 1) * 32]
-            for j in range(JJ):
-                start = (j * 2 + part) * 32
-                near_ref[g, start : start + 32, :] = jnp.where(lane_j == j, rows, 0.0).astype(BF16)
-
-    def one_group(g, _):
-        entries = [blocks_ref[g, k] for k in range(BLOCKS)]
+        near_ref[part] = spread.astype(BF16)
+
+    lane_j = lax.broadcasted_iota(jnp.int32, (32, 256), 1) // 16 % JJ
+    keeps = [jnp.where(lane_j == j, 1.0, 0.0).astype(BF16) for j in range(JJ)]
+
+    for g in range(GROUPS):
+        far_rows = [(blocks_ref[g, k] + g * CG) & (GROUPS * CG - 1) for k in range(BLOCKS)]
         far = jnp.concatenate(
-            [
-                far_ref[pl.ds(pl.multiple_of(((g * G + (e >> 8)) & 63) * CB, CB), CB), :]
-                for e in entries
-            ],
-            axis=0,
+            [far_ref[pl.ds(pl.multiple_of(row, CB), CB), :] for row in far_rows], axis=0
         ).astype(BF16)
-        cross = jnp.dot(far, near_ref[g], preferred_element_type=F32)
-        for k, e in enumerate(entries):
-            near_blk, owner, slot = (e >> 6) & 3, (e >> 1) & 31, e & 1
-            rows = cross[k * CB : (k + 1) * CB]
-            half = jnp.where(near_blk >= 2, rows[:, 128:], rows[:, :128])
-            half = jnp.where((near_blk & 1) != slot, pltpu.roll(half, 64, 1), half)
-            start = pl.multiple_of((g * 32 + owner) * CB, CB)
-            slots_ref[slot, pl.ds(start, CB), :] = half
-        return 0
-
-    lax.fori_loop(0, GROUPS, one_group, 0)
+        sides = [near_ref[side, g * WIN : (g + 1) * WIN, :] for side in range(2)]
+        near = jnp.concatenate([side * keep for keep in keeps for side in sides], axis=0)
+        cross = jnp.dot(far, near, preferred_element_type=F32)
+        for half in range(2):
+            rows = cross[:, half * 128 : (half + 1) * 128]
+            forms_ref[g, half * 256 : (half + 1) * 256, :] = rows
+            forms_ref[g, (half + 2) * 256 : (half + 3) * 256, :] = pltpu.roll(rows, 64, 1)
+        for k in range(BLOCKS):
+            form = pl.multiple_of(blocks_ref[g, BLOCKS + k], CB)
+            place = pl.multiple_of(blocks_ref[g, 2 * BLOCKS + k], CB)
+            slots_ref[g, pl.ds(place, CB), :] = forms_ref[g, pl.ds(form, CB), :]
     first_half = lax.broadcasted_iota(jnp.int32, (256, 128), 1) < 64
-
-    def finish(g, _):
-        rows = pl.ds(pl.multiple_of(g * 256, 256), 256)
-        both = jnp.where(first_half, slots_ref[0, rows, :], slots_ref[1, rows, :])
-        out_ref[rows, :] = both.astype(BF16)
-        return 0
-
-    lax.fori_loop(0, GROUPS, finish, 0)
+    for g in range(GROUPS):
+        low = slots_ref[g, :256, :]
+        high = slots_ref[g, 256:, :]
+        out_ref[g * 256 : (g + 1) * 256, :] = jnp.where(first_half, low, high).astype(BF16)
 
 
 def cross(received, blocks):
@@ -183,8 +173,9 @@
             pltpu.VMEM((GROUPS * WIN * ROWS, 128), F32),
             pltpu.VMEM((512, 256), BF16),
             pltpu.VMEM((512, 256), F32),
-            pltpu.VMEM((GROUPS, 256, 256), BF16),
-            pltpu.VMEM((SLOTS, GROUPS * 32 * CB, 128), F32),
+            pltpu.VMEM((2, 512, 256), BF16),
+            pltpu.VMEM((GROUPS, 4 * 256, 128), F32),
+            pltpu.VMEM((GROUPS, SLOTS * 32 * CB, 128), F32),
         ],
         compiler_params=params(),
     )(received, blocks, near_re, near_im)
@@ -242,9 +233,7 @@
     tiled = spectra.reshape(CG, 2, F // 128, 128).transpose(0, 2, 1, 3).reshape(CG * F // 64, 128)
     sent = whiten(tiled, window_valid, pair_code, block_owner).reshape(PHI, ROWS, 128)
     received = lax.all_to_all(sent, both, 0, 0, tiled=True)
-    fields = received[::WIN, 2].astype(jnp.int32)
-    far, near, owner, rank = (fields[:, i * BLOCKS : (i + 1) * BLOCKS] for i in range(4))
-    blocks = far * 256 + near * 64 + owner * 2 + rank
+    blocks = received[::WIN, 2].astype(jnp.int32) * CB
     crossed = cross(received.reshape(GROUPS * WIN * ROWS, 128), blocks)
     crossed = crossed.reshape(GROUPS * 32, CB, 128)
     arrived = lax.all_to_all(crossed, both, 0, 0, tiled=True).reshape(PHI * CB, 128)

time: 99.3 us -> 96.3 us (0.970)
  Pallas kernels: 9.68 us -> 6.74 us
    pallas_call x1, Pallas kernels: 6.83 us -> 3.92 us  [cross(): pl.pallas_call(cross_kernel, out_shape=jax.ShapeDtypeStruct((GROUPS * 32...]
where the time goes in v3:
time: 96.3 us; the launch traced here: 96.1 us
  blocking collectives  87 us (90%)
  Pallas kernels  6.74 us (7%)
  local copies, waits for them, and re-layouts  1.65 us (2%)
    all_to_all x1, blocking collectives, local(): received = lax.all_to_all(sent, both, 0, 0, tiled=True)  44.4 us
    all_to_all x1, blocking collectives, local(): lax.all_to_all(crossed, both, 0, 0, tiled=True).reshape(PHI * CB, 128)  42.5 us
    pallas_call x1, Pallas kernels, cross(): pl.pallas_call(cross_kernel, out_shape=jax.ShapeDtypeStruct((GROUPS * 32...  3.92 us
    pallas_call x1, Pallas kernels, lags(): pl.pallas_call(lag_kernel, out_shape=jax.ShapeDtypeStruct((SLOTS, CB, CB...  2.11 us

profile of v3, /device:TPU:1, one launch (start us, length us, event | category | flops | bytes accessed | tf_op | source)
XLA Modules:
  0.0 96.1 jit_solution(17324720679319421711)
XLA Ops:
  0.7 0.0 copy-start.6
  0.7 0.0 copy-start.7
  0.7 0.6 copy-done.6
  1.3 0.0 copy-done.7
  1.3 0.0 copy-start.2
  1.3 0.9 copy-done.2
  2.3 0.7 shard_map.91
  3.0 0.0 copy-start.3
  3.0 0.0 copy-start.4
  3.0 44.4 %all_to_all.10 = bf16[512,4,128]{2,1,0:T(4,128)(2,1)S(1)} all-to-all(bf16[512,4,128]{2,1,0:T(4,128)(2,1)S(1)} %bitcast.15), channel_id=1, replica_groups=mesh['chan'=16,'tm'=32] {'chan','tm'}, dimensions={0} | all-to-all | bytes 1048576 | tf_op jit(solution)/shard_map/all_to_all | solution.py:235
  47.5 0.0 copy-done.3
  47.5 0.0 copy-done.4
  47.5 3.9 %shard_map.92 = bf16[4096,128]{1,0:T(8,128)(2,1)S(1)} custom-call(bf16[2048,128]{1,0:T(8,128)(2,1)S(1)} %bitcast.14, s32[16,128]{1,0:T(8,128)S(1)} %multiply_bitcast_fusion.blocks_ref, bf16[256,256]{1,0:T(8,128)(2,1)S(1)} %copy-done.4, bf16[256,256]{1,0:T(8,128)(2,1)S(1)} %copy-done.3), custom_call_target="tpu_custom_call" | custom-call | tf_op jit(solution)/shard_map/pallas_call | solution.py:167
  51.4 0.0 copy-start
  51.5 0.0 copy-start.1
  51.5 0.0 copy-start.5
  51.5 42.5 %all_to_all.11 = bf16[512,8,128]{2,1,0:T(8,128)(2,1)S(1)} all-to-all(bf16[512,8,128]{2,1,0:T(8,128)(2,1)S(1)} %bitcast.12), channel_id=1, replica_groups=mesh['chan'=16,'tm'=32] {'chan','tm'}, dimensions={0} | all-to-all | bytes 2097152 | tf_op jit(solution)/shard_map/all_to_all | solution.py:239
  94.0 0.0 copy-done
  94.0 0.0 copy-done.1
  94.0 0.0 copy-done.5
  94.0 2.1 %shard_map.93 = f32[2,8,2048]{2,1,0:T(8,128)} custom-call(bf16[4096,128]{1,0:T(8,128)(2,1)S(1)} %bitcast.13, bf16[512,512]{1,0:T(8,128)(2,1)S(1)} %copy-done.1, bf16[512,512]{1,0:T(8,128)(2,1)S(1)} %copy-done, f32[16,256]{1,0:T(8,128)S(1)} %copy-done.5), custom_call_target="tpu_custom_call" | custom-call | tf_op jit(solution)/shard_map/pallas_call | solution.py:218
  (2 shorter events, 0.0 us)
Async XLA Ops:
  0.7 0.7 copy-start.6
  0.7 0.7 copy-start.7
  1.3 0.9 copy-start.2
  3.0 44.5 %copy-start.3 = (bf16[256,256]{1,0:T(8,128)(2,1)S(1)}, bf16[256,256]{1,0:T(8,128)(2,1)}, u32[]{:S(2)}) copy-start(bf16[256,256]{1,0:T(8,128)(2,1)} %constant.13.clone.near_im_ref) | copy-start | bytes 393220
  3.0 44.5 %copy-start.4 = (bf16[256,256]{1,0:T(8,128)(2,1)S(1)}, bf16[256,256]{1,0:T(8,128)(2,1)}, u32[]{:S(2)}) copy-start(bf16[256,256]{1,0:T(8,128)(2,1)} %constant.12.clone.near_re_ref) | copy-start | bytes 393220
  51.4 42.6 %copy-start = (bf16[512,512]{1,0:T(8,128)(2,1)S(1)}, bf16[512,512]{1,0:T(8,128)(2,1)}, u32[]{:S(2)}) copy-start(bf16[512,512]{1,0:T(8,128)(2,1)} %constant.15.clone.low_ref) | copy-start | bytes 1572868
  51.5 42.6 %copy-start.1 = (bf16[512,512]{1,0:T(8,128)(2,1)S(1)}, bf16[512,512]{1,0:T(8,128)(2,1)}, u32[]{:S(2)}) copy-start(bf16[512,512]{1,0:T(8,128)(2,1)} %constant.14.clone.high_ref) | copy-start | bytes 1572868
  51.5 42.5 %copy-start.5 = (f32[16,256]{1,0:T(8,128)S(1)}, f32[16,256]{1,0:T(8,128)}, u32[]{:S(2)}) copy-start(f32[16,256]{1,0:T(8,128)} %constant.16.clone.mix_ref) | copy-start | bytes 49156

commit v4 on v3

--- a/solution.py
+++ b/solution.py
@@ -52,8 +52,21 @@
     sent_ref[pl.ds(3, PHI, stride=ROWS), :] = fields
 
 
-def whiten_kernel(x_ref, valid_ref, code_ref, owner_ref, out_ref, wide_ref, sent_ref):
+def whiten_kernel(
+    x_hbm, valid_ref, code_hbm, owner_hbm, out_ref, x_ref, code_ref, owner_ref, wide_ref, sent_ref, sems
+):
+    copies = [
+        pltpu.make_async_copy(source, target, sems.at[i])
+        for i, (source, target) in enumerate(
+            ((x_hbm, x_ref), (code_hbm, code_ref), (owner_hbm, owner_ref))
+        )
+    ]
+    for copy in copies:
+        copy.start()
+    for copy in copies[1:]:
+        copy.wait()
     sent_fields(code_ref, owner_ref, sent_ref)
+    copies[0].wait()
     wide_ref[...] = x_ref[...].astype(F32)
     tiles = F // 128
     raw = [
@@ -79,17 +92,21 @@
 
 
 def whiten(spectra, valid, codes, owners):
-    vmem = pl.BlockSpec(memory_space=pltpu.VMEM)
+    there = pl.BlockSpec(memory_space=pl.ANY)
     return pl.pallas_call(
         whiten_kernel,
         out_shape=jax.ShapeDtypeStruct((PHI * ROWS, 128), BF16),
-        in_specs=[vmem, pl.BlockSpec(memory_space=pltpu.SMEM), vmem, vmem],
-        out_specs=vmem,
+        in_specs=[there, pl.BlockSpec(memory_space=pltpu.SMEM), there, there],
+        out_specs=pl.BlockSpec(memory_space=pltpu.VMEM),
         scratch_shapes=[
+            pltpu.VMEM((CG * F // 64, 128), BF16),
+            pltpu.VMEM((1, BLOCKS), jnp.int32),
+            pltpu.VMEM((1, BLOCKS), jnp.int32),
             pltpu.VMEM((CG * F // 64, 128), F32),
             pltpu.VMEM((PHI * ROWS, 128), F32),
+            pltpu.SemaphoreType.DMA((3,)),
         ],
-        compiler_params=params(),
+        compiler_params=pltpu.CompilerParams(vmem_limit_bytes=62 << 20),
     )(spectra, valid, codes, owners)
 
 

time: 96.3 us -> 96.6 us (level)
  Pallas kernels: 6.74 us -> 8.5 us
  local copies, waits for them, and re-layouts: 1.65 us -> 0.05 us
    pallas_call x1, Pallas kernels: 0.71 us -> 2.46 us  [whiten(): pl.pallas_call(whiten_kernel, out_shape=jax.ShapeDtypeStruct((PHI * ROWS,...]
    unnamed x16 -> x10, local copies, waits for them, and re-layouts: 1.64 us -> 0.03 us
where the time goes in v4:
time: 96.6 us; the launch traced here: 96.4 us
  blocking collectives  87.1 us (90%)
  Pallas kernels  8.5 us (9%)
    all_to_all x1, blocking collectives, local(): received = lax.all_to_all(sent, both, 0, 0, tiled=True)  44.7 us
    all_to_all x1, blocking collectives, local(): lax.all_to_all(crossed, both, 0, 0, tiled=True).reshape(PHI * CB, 128)  42.5 us
    pallas_call x1, Pallas kernels, cross(): pl.pallas_call(cross_kernel, out_shape=jax.ShapeDtypeStruct((GROUPS * 32...  3.92 us
    pallas_call x1, Pallas kernels, whiten(): pl.pallas_call(whiten_kernel, out_shape=jax.ShapeDtypeStruct((PHI * ROWS,...  2.46 us
    pallas_call x1, Pallas kernels, lags(): pl.pallas_call(lag_kernel, out_shape=jax.ShapeDtypeStruct((SLOTS, CB, CB...  2.11 us

profile of v4, /device:TPU:1, one launch (start us, length us, event | category | flops | bytes accessed | tf_op | source)
XLA Modules:
  0.0 96.4 jit_solution(17393555560864699669)
XLA Ops:
  0.7 2.5 %shard_map.91 = bf16[2048,128]{1,0:T(8,128)(2,1)} custom-call(bf16[1024,128]{1,0:T(8,128)(2,1)} %bitcast.16, s32[1]{0:T(128)S(6)} %copy.18.valid_ref, s32[1,32]{1,0:T(1,128)} %code_hbm.1, s32[1,32]{1,0:T(1,128)} %owner_hbm.1), custom_call_target="tpu_custom_call" | custom-call | tf_op jit(solution)/shard_map/pallas_call | solution.py:96
  3.1 0.0 copy-start.2
  3.1 0.0 copy-start.3
  3.1 44.7 %all_to_all.10 = bf16[512,4,128]{2,1,0:T(4,128)(2,1)S(1)} all-to-all(bf16[512,4,128]{2,1,0:T(4,128)(2,1)} %bitcast.15), channel_id=1, replica_groups=mesh['chan'=16,'tm'=32] {'chan','tm'}, dimensions={0} | all-to-all | bytes 1048576 | tf_op jit(solution)/shard_map/all_to_all | solution.py:252
  47.8 0.0 copy-done.2
  47.8 0.0 copy-done.3
  47.9 3.9 %shard_map.92 = bf16[4096,128]{1,0:T(8,128)(2,1)S(1)} custom-call(bf16[2048,128]{1,0:T(8,128)(2,1)S(1)} %bitcast.14, s32[16,128]{1,0:T(8,128)S(1)} %multiply_bitcast_fusion.blocks_ref, bf16[256,256]{1,0:T(8,128)(2,1)S(1)} %copy-done.3, bf16[256,256]{1,0:T(8,128)(2,1)S(1)} %copy-done.2), custom_call_target="tpu_custom_call" | custom-call | tf_op jit(solution)/shard_map/pallas_call | solution.py:184
  51.8 0.0 copy-start
  51.8 0.0 copy-start.1
  51.8 0.0 copy-start.4
  51.8 42.5 %all_to_all.11 = bf16[512,8,128]{2,1,0:T(8,128)(2,1)S(1)} all-to-all(bf16[512,8,128]{2,1,0:T(8,128)(2,1)S(1)} %bitcast.12), channel_id=1, replica_groups=mesh['chan'=16,'tm'=32] {'chan','tm'}, dimensions={0} | all-to-all | bytes 2097152 | tf_op jit(solution)/shard_map/all_to_all | solution.py:256
  94.3 0.0 copy-done
  94.3 0.0 copy-done.1
  94.3 0.0 copy-done.4
  94.3 2.1 %shard_map.93 = f32[2,8,2048]{2,1,0:T(8,128)} custom-call(bf16[4096,128]{1,0:T(8,128)(2,1)S(1)} %bitcast.13, bf16[512,512]{1,0:T(8,128)(2,1)S(1)} %copy-done.1, bf16[512,512]{1,0:T(8,128)(2,1)S(1)} %copy-done, f32[16,256]{1,0:T(8,128)S(1)} %copy-done.4), custom_call_target="tpu_custom_call" | custom-call | tf_op jit(solution)/shard_map/pallas_call | solution.py:235
  (2 shorter events, 0.0 us)
Async XLA Ops:
  3.1 44.7 %copy-start.2 = (bf16[256,256]{1,0:T(8,128)(2,1)S(1)}, bf16[256,256]{1,0:T(8,128)(2,1)}, u32[]{:S(2)}) copy-start(bf16[256,256]{1,0:T(8,128)(2,1)} %constant.13.clone.near_im_ref) | copy-start | bytes 393220
  3.1 44.7 %copy-start.3 = (bf16[256,256]{1,0:T(8,128)(2,1)S(1)}, bf16[256,256]{1,0:T(8,128)(2,1)}, u32[]{:S(2)}) copy-start(bf16[256,256]{1,0:T(8,128)(2,1)} %constant.12.clone.near_re_ref) | copy-start | bytes 393220
  51.8 42.5 %copy-start = (bf16[512,512]{1,0:T(8,128)(2,1)S(1)}, bf16[512,512]{1,0:T(8,128)(2,1)}, u32[]{:S(2)}) copy-start(bf16[512,512]{1,0:T(8,128)(2,1)} %constant.15.clone.low_ref) | copy-start | bytes 1572868
  51.8 42.5 %copy-start.1 = (bf16[512,512]{1,0:T(8,128)(2,1)S(1)}, bf16[512,512]{1,0:T(8,128)(2,1)}, u32[]{:S(2)}) copy-start(bf16[512,512]{1,0:T(8,128)(2,1)} %constant.14.clone.high_ref) | copy-start | bytes 1572868
  51.8 42.5 %copy-start.4 = (f32[16,256]{1,0:T(8,128)S(1)}, f32[16,256]{1,0:T(8,128)}, u32[]{:S(2)}) copy-start(f32[16,256]{1,0:T(8,128)} %constant.16.clone.mix_ref) | copy-start | bytes 49156

commit v5 on v3

--- a/solution.py
+++ b/solution.py
@@ -63,7 +63,7 @@
     squares = sum(block * block for side in raw for block in side)
     mean_power = jnp.sum(squares, axis=1, keepdims=True) * (1.0 / (2 * F))
     scale = lax.rsqrt(mean_power + EPS)
-    valid = valid_ref[0].astype(F32)
+    valid = jnp.broadcast_to(valid_ref[...].astype(F32), (CG, 128))
     for pair in range(JJ // 2):
         for tile in range(PHI // 128):
             rows = jnp.concatenate(
@@ -83,7 +83,7 @@
     return pl.pallas_call(
         whiten_kernel,
         out_shape=jax.ShapeDtypeStruct((PHI * ROWS, 128), BF16),
-        in_specs=[vmem, pl.BlockSpec(memory_space=pltpu.SMEM), vmem, vmem],
+        in_specs=[vmem] * 4,
         out_specs=vmem,
         scratch_shapes=[
             pltpu.VMEM((CG * F // 64, 128), F32),
@@ -231,7 +231,7 @@
 def local(spectra, window_valid, pair_code, block_owner):
     both = ("chan", "tm")
     tiled = spectra.reshape(CG, 2, F // 128, 128).transpose(0, 2, 1, 3).reshape(CG * F // 64, 128)
-    sent = whiten(tiled, window_valid, pair_code, block_owner).reshape(PHI, ROWS, 128)
+    sent = whiten(tiled, window_valid[None], pair_code, block_owner).reshape(PHI, ROWS, 128)
     received = lax.all_to_all(sent, both, 0, 0, tiled=True)
     blocks = received[::WIN, 2].astype(jnp.int32) * CB
     crossed = cross(received.reshape(GROUPS * WIN * ROWS, 128), blocks)

time: 96.3 us -> 96.3 us (level)
  no operation moved by 1% of the time
where the time goes in v5:
time: 96.3 us; the launch traced here: 96.1 us
  blocking collectives  87 us (90%)
  Pallas kernels  6.75 us (7%)
  local copies, waits for them, and re-layouts  1.65 us (2%)
    all_to_all x1, blocking collectives, local(): received = lax.all_to_all(sent, both, 0, 0, tiled=True)  44.4 us
    all_to_all x1, blocking collectives, local(): lax.all_to_all(crossed, both, 0, 0, tiled=True).reshape(PHI * CB, 128)  42.5 us
    pallas_call x1, Pallas kernels, cross(): pl.pallas_call(cross_kernel, out_shape=jax.ShapeDtypeStruct((GROUPS * 32...  3.93 us
    pallas_call x1, Pallas kernels, lags(): pl.pallas_call(lag_kernel, out_shape=jax.ShapeDtypeStruct((SLOTS, CB, CB...  2.12 us

profile of v5, /device:TPU:1, one launch (start us, length us, event | category | flops | bytes accessed | tf_op | source)
XLA Modules:
  0.0 96.1 jit_solution(17676733898975302161)
XLA Ops:
  0.7 0.0 copy-start.6
  0.7 0.0 copy-start.7
  0.7 0.6 copy-done.6
  1.3 0.0 copy-done.7
  1.3 0.0 copy-start.2
  1.3 0.9 copy-done.2
  2.3 0.7 shard_map.91
  3.0 0.0 copy-start.3
  3.0 0.0 copy-start.4
  3.0 44.4 %all_to_all.10 = bf16[512,4,128]{2,1,0:T(4,128)(2,1)S(1)} all-to-all(bf16[512,4,128]{2,1,0:T(4,128)(2,1)S(1)} %bitcast.17), channel_id=1, replica_groups=mesh['chan'=16,'tm'=32] {'chan','tm'}, dimensions={0} | all-to-all | bytes 1048576 | tf_op jit(solution)/shard_map/all_to_all | solution.py:235
  47.5 0.0 copy-done.3
  47.5 0.0 copy-done.4
  47.5 3.9 %shard_map.92 = bf16[4096,128]{1,0:T(8,128)(2,1)S(1)} custom-call(bf16[2048,128]{1,0:T(8,128)(2,1)S(1)} %bitcast.16, s32[16,128]{1,0:T(8,128)S(1)} %multiply_bitcast_fusion.blocks_ref, bf16[256,256]{1,0:T(8,128)(2,1)S(1)} %copy-done.4, bf16[256,256]{1,0:T(8,128)(2,1)S(1)} %copy-done.3), custom_call_target="tpu_custom_call" | custom-call | tf_op jit(solution)/shard_map/pallas_call | solution.py:167
  51.4 0.0 copy-start
  51.5 0.0 copy-start.1
  51.5 0.0 copy-start.5
  51.5 42.5 %all_to_all.11 = bf16[512,8,128]{2,1,0:T(8,128)(2,1)S(1)} all-to-all(bf16[512,8,128]{2,1,0:T(8,128)(2,1)S(1)} %bitcast.14), channel_id=1, replica_groups=mesh['chan'=16,'tm'=32] {'chan','tm'}, dimensions={0} | all-to-all | bytes 2097152 | tf_op jit(solution)/shard_map/all_to_all | solution.py:239
  94.0 0.0 copy-done
  94.0 0.0 copy-done.1
  94.0 0.0 copy-done.5
  94.0 2.1 %shard_map.93 = f32[2,8,2048]{2,1,0:T(8,128)} custom-call(bf16[4096,128]{1,0:T(8,128)(2,1)S(1)} %bitcast.15, bf16[512,512]{1,0:T(8,128)(2,1)S(1)} %copy-done.1, bf16[512,512]{1,0:T(8,128)(2,1)S(1)} %copy-done, f32[16,256]{1,0:T(8,128)S(1)} %copy-done.5), custom_call_target="tpu_custom_call" | custom-call | tf_op jit(solution)/shard_map/pallas_call | solution.py:218
  (2 shorter events, 0.0 us)
Async XLA Ops:
  0.7 0.7 copy-start.6
  0.7 0.7 copy-start.7
  1.3 0.9 copy-start.2
  3.0 44.5 %copy-start.3 = (bf16[256,256]{1,0:T(8,128)(2,1)S(1)}, bf16[256,256]{1,0:T(8,128)(2,1)}, u32[]{:S(2)}) copy-start(bf16[256,256]{1,0:T(8,128)(2,1)} %constant.13.clone.near_im_ref) | copy-start | bytes 393220
  3.0 44.5 %copy-start.4 = (bf16[256,256]{1,0:T(8,128)(2,1)S(1)}, bf16[256,256]{1,0:T(8,128)(2,1)}, u32[]{:S(2)}) copy-start(bf16[256,256]{1,0:T(8,128)(2,1)} %constant.12.clone.near_re_ref) | copy-start | bytes 393220
  51.4 42.6 %copy-start = (bf16[512,512]{1,0:T(8,128)(2,1)S(1)}, bf16[512,512]{1,0:T(8,128)(2,1)}, u32[]{:S(2)}) copy-start(bf16[512,512]{1,0:T(8,128)(2,1)} %constant.15.clone.low_ref) | copy-start | bytes 1572868
  51.5 42.6 %copy-start.1 = (bf16[512,512]{1,0:T(8,128)(2,1)S(1)}, bf16[512,512]{1,0:T(8,128)(2,1)}, u32[]{:S(2)}) copy-start(bf16[512,512]{1,0:T(8,128)(2,1)} %constant.14.clone.high_ref) | copy-start | bytes 1572868
  51.5 42.5 %copy-start.5 = (f32[16,256]{1,0:T(8,128)S(1)}, f32[16,256]{1,0:T(8,128)}, u32[]{:S(2)}) copy-start(f32[16,256]{1,0:T(8,128)} %constant.16.clone.mix_ref) | copy-start | bytes 49156

commit v6 on v3

--- a/solution.py
+++ b/solution.py
@@ -139,7 +139,7 @@
     keeps = [jnp.where(lane_j == j, 1.0, 0.0).astype(BF16) for j in range(JJ)]
 
     for g in range(GROUPS):
-        far_rows = [(blocks_ref[g, k] + g * CG) & (GROUPS * CG - 1) for k in range(BLOCKS)]
+        far_rows = [blocks_ref[g, k] for k in range(BLOCKS)]
         far = jnp.concatenate(
             [far_ref[pl.ds(pl.multiple_of(row, CB), CB), :] for row in far_rows], axis=0
         ).astype(BF16)
@@ -234,6 +234,9 @@
     sent = whiten(tiled, window_valid, pair_code, block_owner).reshape(PHI, ROWS, 128)
     received = lax.all_to_all(sent, both, 0, 0, tiled=True)
     blocks = received[::WIN, 2].astype(jnp.int32) * CB
+    group = jnp.arange(GROUPS, dtype=jnp.int32)[:, None]
+    far = (blocks + group * CG) & (GROUPS * CG - 1)
+    blocks = jnp.where(jnp.arange(128)[None, :] < BLOCKS, far, blocks)
     crossed = cross(received.reshape(GROUPS * WIN * ROWS, 128), blocks)
     crossed = crossed.reshape(GROUPS * 32, CB, 128)
     arrived = lax.all_to_all(crossed, both, 0, 0, tiled=True).reshape(PHI * CB, 128)

time: 96.3 us -> 97.3 us (1.010)
  blocking collectives: 87 us -> 42.5 us
  waiting for transfers between devices: 0 us -> 22.4 us
  starting transfers between devices: 0 us -> 22.2 us
    all_to_all x1 -> x0, blocking collectives: 44.4 us -> none  [local(): received = lax.all_to_all(sent, both, 0, 0, tiled=True)]
    all_to_all x0 -> x1, waiting for transfers between devices: none -> 22.4 us  [local(): received = lax.all_to_all(sent, both, 0, 0, tiled=True)]
    all_to_all x0 -> x1, starting transfers between devices: none -> 22.2 us  [local(): received = lax.all_to_all(sent, both, 0, 0, tiled=True)]
  transfers between devices with their start and end apart: 0 -> 1, of which waited for: 0 -> 1; matrix products, arithmetic and copies ran while one was open for 0% -> 0% of each run, Pallas kernels for 0% -> 0%
where the time goes in v6:
time: 97.3 us; the launch traced here: 97.1 us
  blocking collectives  42.5 us (44%)
  waiting for transfers between devices  22.4 us (23%)
  starting transfers between devices  22.2 us (23%)
  Pallas kernels  7.54 us (8%)
  local copies, waits for them, and re-layouts  1.65 us (2%)
    all_to_all x1, blocking collectives, local(): lax.all_to_all(crossed, both, 0, 0, tiled=True).reshape(PHI * CB, 128)  42.5 us
    all_to_all x1, waiting for transfers between devices, local(): received = lax.all_to_all(sent, both, 0, 0, tiled=True)  22.4 us
    all_to_all x1, starting transfers between devices, local(): received = lax.all_to_all(sent, both, 0, 0, tiled=True)  22.2 us
    pallas_call x1, Pallas kernels, cross(): pl.pallas_call(cross_kernel, out_shape=jax.ShapeDtypeStruct((GROUPS * 32...  3.93 us
    pallas_call x1, Pallas kernels, lags(): pl.pallas_call(lag_kernel, out_shape=jax.ShapeDtypeStruct((SLOTS, CB, CB...  2.11 us
  transfers between devices with their start and end apart: 1, of which 1 were waited for; matrix products, arithmetic and copies ran while one was open for 0% of the time, Pallas kernels for 0%

profile of v6, /device:TPU:1, one launch (start us, length us, event | category | flops | bytes accessed | tf_op | source)
XLA Modules:
  0.0 97.1 jit_solution(4606058426915452028)
XLA Ops:
  0.7 0.0 copy-start.6
  0.7 0.0 copy-start.7
  0.7 0.6 copy-done.6
  1.3 0.0 copy-done.7
  1.3 0.0 copy-start.2
  1.3 0.9 copy-done.2
  2.3 1.5 %shard_map.91 = bf16[2048,128]{1,0:T(8,128)(2,1)} custom-call(bf16[1024,128]{1,0:T(8,128)(2,1)S(1)} %bitcast.20, s32[1]{0:T(128)S(6)} %copy.18.valid_ref, s32[1,32]{1,0:T(1,128)S(1)} %copy-done.6, s32[1,32]{1,0:T(1,128)S(1)} %copy-done.7), custom_call_target="tpu_custom_call" | custom-call | tf_op jit(solution)/shard_map/pallas_call | solution.py:83
  3.8 0.0 copy-start.3
  3.8 0.0 copy-start.4
  3.8 22.2 %all-to-all-start = ((bf16[512,4,128]{2,1,0:T(4,128)(2,1)}), bf16[512,4,128]{2,1,0:T(4,128)(2,1)S(1)}, u32[]{:S(2)}, u32[]{:S(2)}) async-start(bf16[512,4,128]{2,1,0:T(4,128)(2,1)} %bitcast.3), calls=%async_computation | async-start | bytes 1048576 | tf_op jit(solution)/shard_map/all_to_all | solution.py:235
  26.0 22.4 %all-to-all-done = bf16[512,4,128]{2,1,0:T(4,128)(2,1)S(1)} async-done(((bf16[512,4,128]{2,1,0:T(4,128)(2,1)}), bf16[512,4,128]{2,1,0:T(4,128)(2,1)S(1)}, u32[]{:S(2)}, u32[]{:S(2)}) %all-to-all-start) | async-done | bytes 524320 | tf_op jit(solution)/shard_map/all_to_all | solution.py:235
  48.4 0.1 bitcast_select_fusion.blocks_ref
  48.5 0.0 copy-done.3
  48.5 0.0 copy-done.4
  48.5 3.9 %shard_map.92 = bf16[4096,128]{1,0:T(8,128)(2,1)S(1)} custom-call(bf16[2048,128]{1,0:T(8,128)(2,1)S(1)} %bitcast.19, s32[16,128]{1,0:T(8,128)S(1)} %bitcast_select_fusion.blocks_ref, bf16[256,256]{1,0:T(8,128)(2,1)S(1)} %copy-done.4, bf16[256,256]{1,0:T(8,128)(2,1)S(1)} %copy-done.3), custom_call_target="tpu_custom_call" | custom-call | tf_op jit(solution)/shard_map/pallas_call | solution.py:167
  52.5 0.0 copy-start
  52.5 0.0 copy-start.1
  52.5 0.0 copy-start.5
  52.5 42.5 %all_to_all.10 = bf16[512,8,128]{2,1,0:T(8,128)(2,1)S(1)} all-to-all(bf16[512,8,128]{2,1,0:T(8,128)(2,1)S(1)} %bitcast.17), channel_id=1, replica_groups=mesh['chan'=16,'tm'=32] {'chan','tm'}, dimensions={0} | all-to-all | bytes 2097152 | tf_op jit(solution)/shard_map/all_to_all | solution.py:242
  95.0 0.0 copy-done
  95.0 0.0 copy-done.1
  95.0 0.0 copy-done.5
  95.0 2.1 %shard_map.93 = f32[2,8,2048]{2,1,0:T(8,128)} custom-call(bf16[4096,128]{1,0:T(8,128)(2,1)S(1)} %bitcast.18, bf16[512,512]{1,0:T(8,128)(2,1)S(1)} %copy-done.1, bf16[512,512]{1,0:T(8,128)(2,1)S(1)} %copy-done, f32[16,256]{1,0:T(8,128)S(1)} %copy-done.5), custom_call_target="tpu_custom_call" | custom-call | tf_op jit(solution)/shard_map/pallas_call | solution.py:218
  (3 shorter events, 0.0 us)
Async XLA Ops:
  0.7 0.7 copy-start.6
  0.7 0.7 copy-start.7
  1.3 0.9 copy-start.2
  3.8 44.7 %copy-start.3 = (bf16[256,256]{1,0:T(8,128)(2,1)S(1)}, bf16[256,256]{1,0:T(8,128)(2,1)}, u32[]{:S(2)}) copy-start(bf16[256,256]{1,0:T(8,128)(2,1)} %constant.18.clone.near_im_ref) | copy-start | bytes 393220
  3.8 44.7 %copy-start.4 = (bf16[256,256]{1,0:T(8,128)(2,1)S(1)}, bf16[256,256]{1,0:T(8,128)(2,1)}, u32[]{:S(2)}) copy-start(bf16[256,256]{1,0:T(8,128)(2,1)} %constant.7.clone.near_re_ref) | copy-start | bytes 393220
  3.8 44.6 %all-to-all-start = ((bf16[512,4,128]{2,1,0:T(4,128)(2,1)}), bf16[512,4,128]{2,1,0:T(4,128)(2,1)S(1)}, u32[]{:S(2)}, u32[]{:S(2)}) async-start(bf16[512,4,128]{2,1,0:T(4,128)(2,1)} %bitcast.3), calls=%async_computation | async-start | bytes 1048576 | tf_op jit(solution)/shard_map/all_to_all | solution.py:235
  52.5 42.5 %copy-start = (bf16[512,512]{1,0:T(8,128)(2,1)S(1)}, bf16[512,512]{1,0:T(8,128)(2,1)}, u32[]{:S(2)}) copy-start(bf16[512,512]{1,0:T(8,128)(2,1)} %constant.20.clone.low_ref) | copy-start | bytes 1572868
  52.5 42.5 %copy-start.1 = (bf16[512,512]{1,0:T(8,128)(2,1)S(1)}, bf16[512,512]{1,0:T(8,128)(2,1)}, u32[]{:S(2)}) copy-start(bf16[512,512]{1,0:T(8,128)(2,1)} %constant.19.clone.high_ref) | copy-start | bytes 1572868
  52.5 42.5 %copy-start.5 = (f32[16,256]{1,0:T(8,128)S(1)}, f32[16,256]{1,0:T(8,128)}, u32[]{:S(2)}) copy-start(f32[16,256]{1,0:T(8,128)} %constant.21.clone.mix_ref) | copy-start | bytes 49156

commit v7 on v3

--- a/solution.py
+++ b/solution.py
@@ -52,9 +52,8 @@
     sent_ref[pl.ds(3, PHI, stride=ROWS), :] = fields
 
 
-def whiten_kernel(x_ref, valid_ref, code_ref, owner_ref, out_ref, wide_ref, sent_ref):
+def whiten_kernel(wide_ref, valid_ref, code_ref, owner_ref, out_ref, sent_ref):
     sent_fields(code_ref, owner_ref, sent_ref)
-    wide_ref[...] = x_ref[...].astype(F32)
     tiles = F // 128
     raw = [
         [wide_ref[pl.ds(tile * 2 + part, CG, stride=tiles * 2), :] for tile in range(tiles)]
@@ -86,7 +85,6 @@
         in_specs=[vmem, pl.BlockSpec(memory_space=pltpu.SMEM), vmem, vmem],
         out_specs=vmem,
         scratch_shapes=[
-            pltpu.VMEM((CG * F // 64, 128), F32),
             pltpu.VMEM((PHI * ROWS, 128), F32),
         ],
         compiler_params=params(),
@@ -196,21 +194,23 @@
 
 def lag_kernel(m_ref, high_ref, low_ref, mix_ref, out_ref, wide_ref, turned_ref):
     wide_ref[...] = m_ref[...].astype(F32)
-    for far in range(CB):
-        rows = wide_ref[pl.ds(far, PHI, stride=CB), :]
-        turned_ref[far * 128 : (far + 1) * 128, :] = rows.T.astype(BF16)
-    sums = jnp.dot(turned_ref[...], high_ref[...], preferred_element_type=F32)
-    sums = sums + jnp.dot(turned_ref[...], low_ref[...], preferred_element_type=F32)
-    for far in range(CB):
-        for slot in range(SLOTS):
-            total = None
-            for q in range(JJ * 2):
-                start = far * 128 + slot * 64 + q * CB
-                rows = sums[start : start + CB]
-                term = rows[:, :LAGS] * mix_ref[2 * q : 2 * q + 1, :]
-                term = term + rows[:, LAGS:] * mix_ref[2 * q + 1 : 2 * q + 2, :]
-                total = term if total is None else total + term
-            out_ref[slot, :, far * LAGS : (far + 1) * LAGS] = total
+    for far2 in range(CB // 2):
+        rows = jnp.concatenate(
+            [wide_ref[pl.ds(far2 * 2 + half, PHI, stride=CB), :].T for half in range(2)], axis=0
+        ).astype(BF16)
+        sums = jnp.dot(rows, high_ref[...], preferred_element_type=F32)
+        sums = sums + jnp.dot(rows, low_ref[...], preferred_element_type=F32)
+        for half in range(2):
+            far = far2 * 2 + half
+            for slot in range(SLOTS):
+                total = None
+                for q in range(JJ * 2):
+                    start = half * 128 + slot * 64 + q * CB
+                    rows_q = sums[start : start + CB]
+                    term = rows_q[:, :LAGS] * mix_ref[2 * q : 2 * q + 1, :]
+                    term = term + rows_q[:, LAGS:] * mix_ref[2 * q + 1 : 2 * q + 2, :]
+                    total = term if total is None else total + term
+                out_ref[slot, :, far * LAGS : (far + 1) * LAGS] = total
 
 
 def lags(arrived):
@@ -230,7 +230,7 @@
 
 def local(spectra, window_valid, pair_code, block_owner):
     both = ("chan", "tm")
-    tiled = spectra.reshape(CG, 2, F // 128, 128).transpose(0, 2, 1, 3).reshape(CG * F // 64, 128)
+    tiled = spectra.astype(F32).reshape(CG, 2, F // 128, 128).transpose(0, 2, 1, 3).reshape(CG * F // 64, 128)
     sent = whiten(tiled, window_valid, pair_code, block_owner).reshape(PHI, ROWS, 128)
     received = lax.all_to_all(sent, both, 0, 0, tiled=True)
     blocks = received[::WIN, 2].astype(jnp.int32) * CB

time: 96.3 us -> 96.5 us (level)
  other arithmetic: 0.01 us -> 1.24 us
    reshape x0 -> x1, other arithmetic: none -> 1.23 us  [local(): spectra.astype(F32).reshape(CG, 2, F // 128, 128).transpose(0, 2, 1, 3)]
where the time goes in v7:
time: 96.5 us; the launch traced here: 96.3 us
  blocking collectives  87 us (90%)
  Pallas kernels  6.67 us (7%)
  other arithmetic  1.24 us (1%)
    all_to_all x1, blocking collectives, local(): received = lax.all_to_all(sent, both, 0, 0, tiled=True)  44.4 us
    all_to_all x1, blocking collectives, local(): lax.all_to_all(crossed, both, 0, 0, tiled=True).reshape(PHI * CB, 128)  42.5 us
    pallas_call x1, Pallas kernels, cross(): pl.pallas_call(cross_kernel, out_shape=jax.ShapeDtypeStruct((GROUPS * 32...  3.93 us
    pallas_call x1, Pallas kernels, lags(): pl.pallas_call(lag_kernel, out_shape=jax.ShapeDtypeStruct((SLOTS, CB, CB...  2.06 us

profile of v7, /device:TPU:1, one launch (start us, length us, event | category | flops | bytes accessed | tf_op | source)
XLA Modules:
  0.0 96.3 jit_solution(7644066337635289660)
XLA Ops:
  0.7 1.2 %bitcast_convert_fusion = f32[32,2,16,128]{3,1,2,0:T(2,128)S(1)} fusion(bf16[1,32,2,2048]{3,2,1,0:T(2,128)(2,1)} %param.9), kind=kLoop, calls=%fused_computation | loop fusion | flops 131072 | bytes 786432 | tf_op jit(solution)/shard_map/reshape | solution.py:233
  1.9 0.0 copy-start.5
  1.9 0.0 copy-start.6
  1.9 0.6 copy-done.5
  2.5 0.0 copy-done.6
  2.6 0.7 shard_map.91
  3.3 0.0 copy-start.2
  3.3 0.0 copy-start.3
  3.3 44.4 %all_to_all.10 = bf16[512,4,128]{2,1,0:T(4,128)(2,1)S(1)} all-to-all(bf16[512,4,128]{2,1,0:T(4,128)(2,1)S(1)} %bitcast.16), channel_id=1, replica_groups=mesh['chan'=16,'tm'=32] {'chan','tm'}, dimensions={0} | all-to-all | bytes 1048576 | tf_op jit(solution)/shard_map/all_to_all | solution.py:235
  47.8 0.0 copy-done.2
  47.8 0.0 copy-done.3
  47.8 3.9 %shard_map.92 = bf16[4096,128]{1,0:T(8,128)(2,1)S(1)} custom-call(bf16[2048,128]{1,0:T(8,128)(2,1)S(1)} %bitcast.15, s32[16,128]{1,0:T(8,128)S(1)} %multiply_bitcast_fusion.blocks_ref, bf16[256,256]{1,0:T(8,128)(2,1)S(1)} %copy-done.3, bf16[256,256]{1,0:T(8,128)(2,1)S(1)} %copy-done.2), custom_call_target="tpu_custom_call" | custom-call | tf_op jit(solution)/shard_map/pallas_call | solution.py:165
  51.7 0.0 copy-start
  51.7 0.0 copy-start.1
  51.7 0.0 copy-start.4
  51.7 42.5 %all_to_all.11 = bf16[512,8,128]{2,1,0:T(8,128)(2,1)S(1)} all-to-all(bf16[512,8,128]{2,1,0:T(8,128)(2,1)S(1)} %bitcast.13), channel_id=1, replica_groups=mesh['chan'=16,'tm'=32] {'chan','tm'}, dimensions={0} | all-to-all | bytes 2097152 | tf_op jit(solution)/shard_map/all_to_all | solution.py:239
  94.3 0.0 copy-done
  94.3 0.0 copy-done.1
  94.3 0.0 copy-done.4
  94.3 2.1 %shard_map.93 = f32[2,8,2048]{2,1,0:T(8,128)} custom-call(bf16[4096,128]{1,0:T(8,128)(2,1)S(1)} %bitcast.14, bf16[512,512]{1,0:T(8,128)(2,1)S(1)} %copy-done.1, bf16[512,512]{1,0:T(8,128)(2,1)S(1)} %copy-done, f32[16,256]{1,0:T(8,128)S(1)} %copy-done.4), custom_call_target="tpu_custom_call" | custom-call | tf_op jit(solution)/shard_map/pallas_call | solution.py:218
  (2 shorter events, 0.0 us)
Async XLA Ops:
  1.9 0.7 copy-start.5
  1.9 0.7 copy-start.6
  3.3 44.5 %copy-start.2 = (bf16[256,256]{1,0:T(8,128)(2,1)S(1)}, bf16[256,256]{1,0:T(8,128)(2,1)}, u32[]{:S(2)}) copy-start(bf16[256,256]{1,0:T(8,128)(2,1)} %constant.13.clone.near_im_ref) | copy-start | bytes 393220
  3.3 44.5 %copy-start.3 = (bf16[256,256]{1,0:T(8,128)(2,1)S(1)}, bf16[256,256]{1,0:T(8,128)(2,1)}, u32[]{:S(2)}) copy-start(bf16[256,256]{1,0:T(8,128)(2,1)} %constant.12.clone.near_re_ref) | copy-start | bytes 393220
  51.7 42.6 %copy-start = (bf16[512,512]{1,0:T(8,128)(2,1)S(1)}, bf16[512,512]{1,0:T(8,128)(2,1)}, u32[]{:S(2)}) copy-start(bf16[512,512]{1,0:T(8,128)(2,1)} %constant.15.clone.low_ref) | copy-start | bytes 1572868
  51.7 42.6 %copy-start.1 = (bf16[512,512]{1,0:T(8,128)(2,1)S(1)}, bf16[512,512]{1,0:T(8,128)(2,1)}, u32[]{:S(2)}) copy-start(bf16[512,512]{1,0:T(8,128)(2,1)} %constant.14.clone.high_ref) | copy-start | bytes 1572868
  51.7 42.5 %copy-start.4 = (f32[16,256]{1,0:T(8,128)S(1)}, f32[16,256]{1,0:T(8,128)}, u32[]{:S(2)}) copy-start(f32[16,256]{1,0:T(8,128)} %constant.16.clone.mix_ref) | copy-start | bytes 49156

commit v8 on v3

--- a/solution.py
+++ b/solution.py
@@ -31,7 +31,7 @@
     return pltpu.CompilerParams(vmem_limit_bytes=40 << 20)
 
 
-def sent_fields(code_ref, owner_ref, sent_ref):
+def fields_kernel(code_ref, owner_ref, out_ref):
     lane = lax.broadcasted_iota(jnp.int32, (1, 128), 1)
     fill = jnp.full((1, 128 - BLOCKS), -1, jnp.int32)
     owner = jnp.concatenate([owner_ref[...], fill], axis=1)
@@ -47,13 +47,13 @@
     fields = jnp.where(lane < BLOCKS, far, pltpu.roll(form, BLOCKS, 1))
     fields = jnp.where(lane < 2 * BLOCKS, fields, pltpu.roll(place, 2 * BLOCKS, 1))
     fields = jnp.where(lane < 3 * BLOCKS, fields, 0)
-    fields = jnp.broadcast_to(fields.astype(F32), (PHI, 128))
+    out_ref[...] = fields.astype(F32)
+
+
+def whiten_kernel(x_ref, valid_ref, fields_ref, out_ref, wide_ref, sent_ref):
+    fields = jnp.broadcast_to(fields_ref[...], (PHI, 128))
     sent_ref[pl.ds(2, PHI, stride=ROWS), :] = fields
     sent_ref[pl.ds(3, PHI, stride=ROWS), :] = fields
-
-
-def whiten_kernel(x_ref, valid_ref, code_ref, owner_ref, out_ref, wide_ref, sent_ref):
-    sent_fields(code_ref, owner_ref, sent_ref)
     wide_ref[...] = x_ref[...].astype(F32)
     tiles = F // 128
     raw = [
@@ -80,17 +80,25 @@
 
 def whiten(spectra, valid, codes, owners):
     vmem = pl.BlockSpec(memory_space=pltpu.VMEM)
+    fields = pl.pallas_call(
+        fields_kernel,
+        out_shape=jax.ShapeDtypeStruct((1, 128), F32),
+        in_specs=[vmem] * 2,
+        out_specs=vmem,
+        compiler_params=params(),
+        cost_estimate=pl.CostEstimate(flops=1 << 22, bytes_accessed=1 << 20, transcendentals=0),
+    )(codes, owners)
     return pl.pallas_call(
         whiten_kernel,
         out_shape=jax.ShapeDtypeStruct((PHI * ROWS, 128), BF16),
-        in_specs=[vmem, pl.BlockSpec(memory_space=pltpu.SMEM), vmem, vmem],
+        in_specs=[vmem, pl.BlockSpec(memory_space=pltpu.SMEM), vmem],
         out_specs=vmem,
         scratch_shapes=[
             pltpu.VMEM((CG * F // 64, 128), F32),
             pltpu.VMEM((PHI * ROWS, 128), F32),
         ],
         compiler_params=params(),
-    )(spectra, valid, codes, owners)
+    )(spectra, valid, fields)
 
 
 def near_tables():

time: 96.3 us -> 95.9 us (level)
  no operation moved by 1% of the time
where the time goes in v8:
time: 95.9 us; the launch traced here: 95.7 us
  blocking collectives  87 us (91%)
  Pallas kernels  6.89 us (7%)
  local copies, waits for them, and re-layouts  1.01 us (1%)
    all_to_all x1, blocking collectives, local(): received = lax.all_to_all(sent, both, 0, 0, tiled=True)  44.4 us
    all_to_all x1, blocking collectives, local(): lax.all_to_all(crossed, both, 0, 0, tiled=True).reshape(PHI * CB, 128)  42.5 us
    pallas_call x1, Pallas kernels, cross(): pl.pallas_call(cross_kernel, out_shape=jax.ShapeDtypeStruct((GROUPS * 32...  3.93 us
    pallas_call x1, Pallas kernels, lags(): pl.pallas_call(lag_kernel, out_shape=jax.ShapeDtypeStruct((SLOTS, CB, CB...  2.11 us

profile of v8, /device:TPU:1, one launch (start us, length us, event | category | flops | bytes accessed | tf_op | source)
XLA Modules:
  0.0 95.7 jit_solution(14593989588539292833)
XLA Ops:
  0.0 0.0 copy-start.7
  0.0 0.0 copy-start.6
  0.7 0.0 copy-done.7
  0.7 0.0 copy-done.6
  0.7 0.2 shard_map.91.fields_ref
  0.9 0.0 copy-start.2
  0.9 1.0 copy-done.2
  1.8 0.7 shard_map.92
  2.5 0.0 copy-start.3
  2.5 0.0 copy-start.4
  2.6 44.4 %all_to_all.10 = bf16[512,4,128]{2,1,0:T(4,128)(2,1)S(1)} all-to-all(bf16[512,4,128]{2,1,0:T(4,128)(2,1)S(1)} %bitcast.15), channel_id=1, replica_groups=mesh['chan'=16,'tm'=32] {'chan','tm'}, dimensions={0} | all-to-all | bytes 1048576 | tf_op jit(solution)/shard_map/all_to_all | solution.py:243
  47.0 0.0 copy-done.3
  47.0 0.0 copy-done.4
  47.0 3.9 %shard_map.93 = bf16[4096,128]{1,0:T(8,128)(2,1)S(1)} custom-call(bf16[2048,128]{1,0:T(8,128)(2,1)S(1)} %bitcast.14, s32[16,128]{1,0:T(8,128)S(1)} %multiply_bitcast_fusion.blocks_ref, bf16[256,256]{1,0:T(8,128)(2,1)S(1)} %copy-done.4, bf16[256,256]{1,0:T(8,128)(2,1)S(1)} %copy-done.3), custom_call_target="tpu_custom_call" | custom-call | tf_op jit(solution)/shard_map/pallas_call | solution.py:175
  51.0 0.0 copy-start
  51.0 0.0 copy-start.1
  51.0 0.0 copy-start.5
  51.0 42.5 %all_to_all.11 = bf16[512,8,128]{2,1,0:T(8,128)(2,1)S(1)} all-to-all(bf16[512,8,128]{2,1,0:T(8,128)(2,1)S(1)} %bitcast.12), channel_id=1, replica_groups=mesh['chan'=16,'tm'=32] {'chan','tm'}, dimensions={0} | all-to-all | bytes 2097152 | tf_op jit(solution)/shard_map/all_to_all | solution.py:247
  93.5 0.0 copy-done
  93.5 0.0 copy-done.1
  93.6 0.0 copy-done.5
  93.6 2.1 %shard_map.94 = f32[2,8,2048]{2,1,0:T(8,128)} custom-call(bf16[4096,128]{1,0:T(8,128)(2,1)S(1)} %bitcast.13, bf16[512,512]{1,0:T(8,128)(2,1)S(1)} %copy-done.1, bf16[512,512]{1,0:T(8,128)(2,1)S(1)} %copy-done, f32[16,256]{1,0:T(8,128)S(1)} %copy-done.5), custom_call_target="tpu_custom_call" | custom-call | tf_op jit(solution)/shard_map/pallas_call | solution.py:226
  (2 shorter events, 0.0 us)
Async XLA Ops:
  0.0 0.7 copy-start.7
  0.0 0.7 copy-start.6
  0.9 1.0 %copy-start.2 = (bf16[1,32,2,2048]{3,2,1,0:T(2,128)(2,1)S(1)}, bf16[1,32,2,2048]{3,2,1,0:T(2,128)(2,1)}, u32[]{:S(2)}) copy-start(bf16[1,32,2,2048]{3,2,1,0:T(2,128)(2,1)} %param.9) | copy-start | bytes 786436
  2.5 44.5 %copy-start.3 = (bf16[256,256]{1,0:T(8,128)(2,1)S(1)}, bf16[256,256]{1,0:T(8,128)(2,1)}, u32[]{:S(2)}) copy-start(bf16[256,256]{1,0:T(8,128)(2,1)} %constant.13.clone.near_im_ref) | copy-start | bytes 393220
  2.5 44.5 %copy-start.4 = (bf16[256,256]{1,0:T(8,128)(2,1)S(1)}, bf16[256,256]{1,0:T(8,128)(2,1)}, u32[]{:S(2)}) copy-start(bf16[256,256]{1,0:T(8,128)(2,1)} %constant.12.clone.near_re_ref) | copy-start | bytes 393220
  51.0 42.6 %copy-start = (bf16[512,512]{1,0:T(8,128)(2,1)S(1)}, bf16[512,512]{1,0:T(8,128)(2,1)}, u32[]{:S(2)}) copy-start(bf16[512,512]{1,0:T(8,128)(2,1)} %constant.15.clone.low_ref) | copy-start | bytes 1572868
  51.0 42.6 %copy-start.1 = (bf16[512,512]{1,0:T(8,128)(2,1)S(1)}, bf16[512,512]{1,0:T(8,128)(2,1)}, u32[]{:S(2)}) copy-start(bf16[512,512]{1,0:T(8,128)(2,1)} %constant.14.clone.high_ref) | copy-start | bytes 1572868
  51.0 42.5 %copy-start.5 = (f32[16,256]{1,0:T(8,128)S(1)}, f32[16,256]{1,0:T(8,128)}, u32[]{:S(2)}) copy-start(f32[16,256]{1,0:T(8,128)} %constant.16.clone.mix_ref) | copy-start | bytes 49156

commit v9 on v7

--- a/solution.py
+++ b/solution.py
@@ -31,7 +31,7 @@
     return pltpu.CompilerParams(vmem_limit_bytes=40 << 20)
 
 
-def sent_fields(code_ref, owner_ref, sent_ref):
+def fields_kernel(code_ref, owner_ref, out_ref):
     lane = lax.broadcasted_iota(jnp.int32, (1, 128), 1)
     fill = jnp.full((1, 128 - BLOCKS), -1, jnp.int32)
     owner = jnp.concatenate([owner_ref[...], fill], axis=1)
@@ -47,13 +47,14 @@
     fields = jnp.where(lane < BLOCKS, far, pltpu.roll(form, BLOCKS, 1))
     fields = jnp.where(lane < 2 * BLOCKS, fields, pltpu.roll(place, 2 * BLOCKS, 1))
     fields = jnp.where(lane < 3 * BLOCKS, fields, 0)
-    fields = jnp.broadcast_to(fields.astype(F32), (PHI, 128))
+    out_ref[...] = fields.astype(F32)
+
+
+def whiten_kernel(x_ref, valid_ref, fields_ref, out_ref, wide_ref, sent_ref):
+    fields = jnp.broadcast_to(fields_ref[...], (PHI, 128))
     sent_ref[pl.ds(2, PHI, stride=ROWS), :] = fields
     sent_ref[pl.ds(3, PHI, stride=ROWS), :] = fields
-
-
-def whiten_kernel(wide_ref, valid_ref, code_ref, owner_ref, out_ref, sent_ref):
-    sent_fields(code_ref, owner_ref, sent_ref)
+    wide_ref[...] = x_ref[...].astype(F32)
     tiles = F // 128
     raw = [
         [wide_ref[pl.ds(tile * 2 + part, CG, stride=tiles * 2), :] for tile in range(tiles)]
@@ -79,16 +80,25 @@
 
 def whiten(spectra, valid, codes, owners):
     vmem = pl.BlockSpec(memory_space=pltpu.VMEM)
+    fields = pl.pallas_call(
+        fields_kernel,
+        out_shape=jax.ShapeDtypeStruct((1, 128), F32),
+        in_specs=[vmem] * 2,
+        out_specs=vmem,
+        compiler_params=params(),
+        cost_estimate=pl.CostEstimate(flops=1 << 22, bytes_accessed=1 << 20, transcendentals=0),
+    )(codes, owners)
     return pl.pallas_call(
         whiten_kernel,
         out_shape=jax.ShapeDtypeStruct((PHI * ROWS, 128), BF16),
-        in_specs=[vmem, pl.BlockSpec(memory_space=pltpu.SMEM), vmem, vmem],
+        in_specs=[vmem, pl.BlockSpec(memory_space=pltpu.SMEM), vmem],
         out_specs=vmem,
         scratch_shapes=[
+            pltpu.VMEM((CG * F // 64, 128), F32),
             pltpu.VMEM((PHI * ROWS, 128), F32),
         ],
         compiler_params=params(),
-    )(spectra, valid, codes, owners)
+    )(spectra, valid, fields)
 
 
 def near_tables():
@@ -192,7 +202,7 @@
     return high, low, mix.astype(np.float32)
 
 
-def lag_kernel(m_ref, high_ref, low_ref, mix_ref, out_ref, wide_ref, turned_ref):
+def lag_kernel(m_ref, high_ref, low_ref, mix_ref, out_ref, wide_ref):
     wide_ref[...] = m_ref[...].astype(F32)
     for far2 in range(CB // 2):
         rows = jnp.concatenate(
@@ -222,7 +232,6 @@
         out_specs=pl.BlockSpec(memory_space=pltpu.VMEM),
         scratch_shapes=[
             pltpu.VMEM((PHI * CB, 128), F32),
-            pltpu.VMEM((CB * 128, PHI), BF16),
         ],
         compiler_params=params(),
     )(arrived, jnp.asarray(high), jnp.asarray(low), jnp.asarray(mix))
@@ -230,7 +239,7 @@
 
 def local(spectra, window_valid, pair_code, block_owner):
     both = ("chan", "tm")
-    tiled = spectra.astype(F32).reshape(CG, 2, F // 128, 128).transpose(0, 2, 1, 3).reshape(CG * F // 64, 128)
+    tiled = spectra.reshape(CG, 2, F // 128, 128).transpose(0, 2, 1, 3).reshape(CG * F // 64, 128)
     sent = whiten(tiled, window_valid, pair_code, block_owner).reshape(PHI, ROWS, 128)
     received = lax.all_to_all(sent, both, 0, 0, tiled=True)
     blocks = received[::WIN, 2].astype(jnp.int32) * CB

time: 96.5 us -> 95.8 us (level)
  other arithmetic: 1.24 us -> 0.01 us
    reshape x1 -> x0, other arithmetic: 1.23 us -> none  [local(): spectra.astype(F32).reshape(CG, 2, F // 128, 128).transpose(0, 2, 1, 3)]
where the time goes in v9:
time: 95.8 us; the launch traced here: 95.6 us
  blocking collectives  87 us (91%)
  Pallas kernels  6.85 us (7%)
  local copies, waits for them, and re-layouts  1.01 us (1%)
    all_to_all x1, blocking collectives, local(): received = lax.all_to_all(sent, both, 0, 0, tiled=True)  44.4 us
    all_to_all x1, blocking collectives, local(): lax.all_to_all(crossed, both, 0, 0, tiled=True).reshape(PHI * CB, 128)  42.5 us
    pallas_call x1, Pallas kernels, cross(): pl.pallas_call(cross_kernel, out_shape=jax.ShapeDtypeStruct((GROUPS * 32...  3.93 us
    pallas_call x1, Pallas kernels, lags(): pl.pallas_call(lag_kernel, out_shape=jax.ShapeDtypeStruct((SLOTS, CB, CB...  2.06 us

profile of v9, /device:TPU:1, one launch (start us, length us, event | category | flops | bytes accessed | tf_op | source)
XLA Modules:
  0.0 95.6 jit_solution(847507732979020603)
XLA Ops:
  0.0 0.0 copy-start.7
  0.0 0.0 copy-start.6
  0.7 0.0 copy-done.7
  0.7 0.0 copy-done.6
  0.7 0.2 shard_map.91.fields_ref
  0.9 0.0 copy-start.2
  0.9 1.0 %copy-done.2 = bf16[1,32,2,2048]{3,2,1,0:T(2,128)(2,1)S(1)} copy-done((bf16[1,32,2,2048]{3,2,1,0:T(2,128)(2,1)S(1)}, bf16[1,32,2,2048]{3,2,1,0:T(2,128)(2,1)}, u32[]{:S(2)}) %copy-start.2) | copy-done | bytes 262168
  1.8 0.7 shard_map.92
  2.5 0.0 copy-start.3
  2.5 0.0 copy-start.4
  2.6 44.4 %all_to_all.10 = bf16[512,4,128]{2,1,0:T(4,128)(2,1)S(1)} all-to-all(bf16[512,4,128]{2,1,0:T(4,128)(2,1)S(1)} %bitcast.15), channel_id=1, replica_groups=mesh['chan'=16,'tm'=32] {'chan','tm'}, dimensions={0} | all-to-all | bytes 1048576 | tf_op jit(solution)/shard_map/all_to_all | solution.py:244
  47.0 0.0 copy-done.3
  47.0 0.0 copy-done.4
  47.0 3.9 %shard_map.93 = bf16[4096,128]{1,0:T(8,128)(2,1)S(1)} custom-call(bf16[2048,128]{1,0:T(8,128)(2,1)S(1)} %bitcast.14, s32[16,128]{1,0:T(8,128)S(1)} %multiply_bitcast_fusion.blocks_ref, bf16[256,256]{1,0:T(8,128)(2,1)S(1)} %copy-done.4, bf16[256,256]{1,0:T(8,128)(2,1)S(1)} %copy-done.3), custom_call_target="tpu_custom_call" | custom-call | tf_op jit(solution)/shard_map/pallas_call | solution.py:175
  51.0 0.0 copy-start
  51.0 0.0 copy-start.1
  51.0 0.0 copy-start.5
  51.0 42.5 %all_to_all.11 = bf16[512,8,128]{2,1,0:T(8,128)(2,1)S(1)} all-to-all(bf16[512,8,128]{2,1,0:T(8,128)(2,1)S(1)} %bitcast.12), channel_id=1, replica_groups=mesh['chan'=16,'tm'=32] {'chan','tm'}, dimensions={0} | all-to-all | bytes 2097152 | tf_op jit(solution)/shard_map/all_to_all | solution.py:248
  93.5 0.0 copy-done
  93.6 0.0 copy-done.1
  93.6 0.0 copy-done.5
  93.6 2.1 %shard_map.94 = f32[2,8,2048]{2,1,0:T(8,128)} custom-call(bf16[4096,128]{1,0:T(8,128)(2,1)S(1)} %bitcast.13, bf16[512,512]{1,0:T(8,128)(2,1)S(1)} %copy-done.1, bf16[512,512]{1,0:T(8,128)(2,1)S(1)} %copy-done, f32[16,256]{1,0:T(8,128)S(1)} %copy-done.5), custom_call_target="tpu_custom_call" | custom-call | tf_op jit(solution)/shard_map/pallas_call | solution.py:228
  (2 shorter events, 0.0 us)
Async XLA Ops:
  0.0 0.7 copy-start.7
  0.0 0.7 copy-start.6
  0.9 1.0 %copy-start.2 = (bf16[1,32,2,2048]{3,2,1,0:T(2,128)(2,1)S(1)}, bf16[1,32,2,2048]{3,2,1,0:T(2,128)(2,1)}, u32[]{:S(2)}) copy-start(bf16[1,32,2,2048]{3,2,1,0:T(2,128)(2,1)} %param.9) | copy-start | bytes 786436
  2.5 44.5 %copy-start.3 = (bf16[256,256]{1,0:T(8,128)(2,1)S(1)}, bf16[256,256]{1,0:T(8,128)(2,1)}, u32[]{:S(2)}) copy-start(bf16[256,256]{1,0:T(8,128)(2,1)} %constant.13.clone.near_im_ref) | copy-start | bytes 393220
  2.5 44.5 %copy-start.4 = (bf16[256,256]{1,0:T(8,128)(2,1)S(1)}, bf16[256,256]{1,0:T(8,128)(2,1)}, u32[]{:S(2)}) copy-start(bf16[256,256]{1,0:T(8,128)(2,1)} %constant.12.clone.near_re_ref) | copy-start | bytes 393220
  51.0 42.6 %copy-start = (bf16[512,512]{1,0:T(8,128)(2,1)S(1)}, bf16[512,512]{1,0:T(8,128)(2,1)}, u32[]{:S(2)}) copy-start(bf16[512,512]{1,0:T(8,128)(2,1)} %constant.15.clone.low_ref) | copy-start | bytes 1572868
  51.0 42.6 %copy-start.1 = (bf16[512,512]{1,0:T(8,128)(2,1)S(1)}, bf16[512,512]{1,0:T(8,128)(2,1)}, u32[]{:S(2)}) copy-start(bf16[512,512]{1,0:T(8,128)(2,1)} %constant.14.clone.high_ref) | copy-start | bytes 1572868
  51.0 42.5 %copy-start.5 = (f32[16,256]{1,0:T(8,128)S(1)}, f32[16,256]{1,0:T(8,128)}, u32[]{:S(2)}) copy-start(f32[16,256]{1,0:T(8,128)} %constant.16.clone.mix_ref) | copy-start | bytes 49156

commit v10 on v9

--- a/solution.py
+++ b/solution.py
@@ -121,7 +121,6 @@
 def cross_kernel(
     r_ref, blocks_ref, near_re_ref, near_im_ref, out_ref, wide_ref, own_ref, far_ref, near_ref, forms_ref, slots_ref
 ):
-    slots_ref[...] = jnp.zeros_like(slots_ref)
     wide_ref[...] = r_ref[...].astype(F32)
     quarter = lax.broadcasted_iota(jnp.int32, (32, 128), 1) // 32
     for g4 in range(GROUPS // 4):
@@ -147,6 +146,7 @@
     keeps = [jnp.where(lane_j == j, 1.0, 0.0).astype(BF16) for j in range(JJ)]
 
     for g in range(GROUPS):
+        slots_ref[g] = jnp.zeros((SLOTS * 32 * CB, 128), F32)
         far_rows = [(blocks_ref[g, k] + g * CG) & (GROUPS * CG - 1) for k in range(BLOCKS)]
         far = jnp.concatenate(
             [far_ref[pl.ds(pl.multiple_of(row, CB), CB), :] for row in far_rows], axis=0

time: 95.8 us -> 95.7 us (level)
  no operation moved by 1% of the time
where the time goes in v10:
time: 95.7 us; the launch traced here: 95.5 us
  blocking collectives  87 us (91%)
  Pallas kernels  6.7 us (7%)
  local copies, waits for them, and re-layouts  1.01 us (1%)
    all_to_all x1, blocking collectives, local(): received = lax.all_to_all(sent, both, 0, 0, tiled=True)  44.4 us
    all_to_all x1, blocking collectives, local(): lax.all_to_all(crossed, both, 0, 0, tiled=True).reshape(PHI * CB, 128)  42.5 us
    pallas_call x1, Pallas kernels, cross(): pl.pallas_call(cross_kernel, out_shape=jax.ShapeDtypeStruct((GROUPS * 32...  3.78 us
    pallas_call x1, Pallas kernels, lags(): pl.pallas_call(lag_kernel, out_shape=jax.ShapeDtypeStruct((SLOTS, CB, CB...  2.06 us

profile of v10, /device:TPU:1, one launch (start us, length us, event | category | flops | bytes accessed | tf_op | source)
XLA Modules:
  0.0 95.5 jit_solution(18179978866976466472)
XLA Ops:
  0.0 0.0 copy-start.7
  0.0 0.0 copy-start.6
  0.7 0.0 copy-done.7
  0.7 0.0 copy-done.6
  0.7 0.2 shard_map.91.fields_ref
  0.9 0.0 copy-start.2
  0.9 1.0 %copy-done.2 = bf16[1,32,2,2048]{3,2,1,0:T(2,128)(2,1)S(1)} copy-done((bf16[1,32,2,2048]{3,2,1,0:T(2,128)(2,1)S(1)}, bf16[1,32,2,2048]{3,2,1,0:T(2,128)(2,1)}, u32[]{:S(2)}) %copy-start.2) | copy-done | bytes 262168
  1.8 0.7 shard_map.92
  2.5 0.0 copy-start.3
  2.5 0.0 copy-start.4
  2.6 44.4 %all_to_all.10 = bf16[512,4,128]{2,1,0:T(4,128)(2,1)S(1)} all-to-all(bf16[512,4,128]{2,1,0:T(4,128)(2,1)S(1)} %bitcast.15), channel_id=1, replica_groups=mesh['chan'=16,'tm'=32] {'chan','tm'}, dimensions={0} | all-to-all | bytes 1048576 | tf_op jit(solution)/shard_map/all_to_all | solution.py:244
  47.0 0.0 copy-done.3
  47.0 0.0 copy-done.4
  47.0 3.8 %shard_map.93 = bf16[4096,128]{1,0:T(8,128)(2,1)S(1)} custom-call(bf16[2048,128]{1,0:T(8,128)(2,1)S(1)} %bitcast.14, s32[16,128]{1,0:T(8,128)S(1)} %multiply_bitcast_fusion.blocks_ref, bf16[256,256]{1,0:T(8,128)(2,1)S(1)} %copy-done.4, bf16[256,256]{1,0:T(8,128)(2,1)S(1)} %copy-done.3), custom_call_target="tpu_custom_call" | custom-call | tf_op jit(solution)/shard_map/pallas_call | solution.py:175
  50.8 0.0 copy-start
  50.8 0.0 copy-start.1
  50.9 0.0 copy-start.5
  50.9 42.5 %all_to_all.11 = bf16[512,8,128]{2,1,0:T(8,128)(2,1)S(1)} all-to-all(bf16[512,8,128]{2,1,0:T(8,128)(2,1)S(1)} %bitcast.12), channel_id=1, replica_groups=mesh['chan'=16,'tm'=32] {'chan','tm'}, dimensions={0} | all-to-all | bytes 2097152 | tf_op jit(solution)/shard_map/all_to_all | solution.py:248
  93.4 0.0 copy-done
  93.4 0.0 copy-done.1
  93.4 0.0 copy-done.5
  93.4 2.1 %shard_map.94 = f32[2,8,2048]{2,1,0:T(8,128)} custom-call(bf16[4096,128]{1,0:T(8,128)(2,1)S(1)} %bitcast.13, bf16[512,512]{1,0:T(8,128)(2,1)S(1)} %copy-done.1, bf16[512,512]{1,0:T(8,128)(2,1)S(1)} %copy-done, f32[16,256]{1,0:T(8,128)S(1)} %copy-done.5), custom_call_target="tpu_custom_call" | custom-call | tf_op jit(solution)/shard_map/pallas_call | solution.py:228
  (2 shorter events, 0.0 us)
Async XLA Ops:
  0.0 0.7 copy-start.7
  0.0 0.7 copy-start.6
  0.9 1.0 %copy-start.2 = (bf16[1,32,2,2048]{3,2,1,0:T(2,128)(2,1)S(1)}, bf16[1,32,2,2048]{3,2,1,0:T(2,128)(2,1)}, u32[]{:S(2)}) copy-start(bf16[1,32,2,2048]{3,2,1,0:T(2,128)(2,1)} %param.9) | copy-start | bytes 786436
  2.5 44.5 %copy-start.3 = (bf16[256,256]{1,0:T(8,128)(2,1)S(1)}, bf16[256,256]{1,0:T(8,128)(2,1)}, u32[]{:S(2)}) copy-start(bf16[256,256]{1,0:T(8,128)(2,1)} %constant.13.clone.near_im_ref) | copy-start | bytes 393220
  2.5 44.5 %copy-start.4 = (bf16[256,256]{1,0:T(8,128)(2,1)S(1)}, bf16[256,256]{1,0:T(8,128)(2,1)}, u32[]{:S(2)}) copy-start(bf16[256,256]{1,0:T(8,128)(2,1)} %constant.12.clone.near_re_ref) | copy-start | bytes 393220
  50.8 42.6 %copy-start = (bf16[512,512]{1,0:T(8,128)(2,1)S(1)}, bf16[512,512]{1,0:T(8,128)(2,1)}, u32[]{:S(2)}) copy-start(bf16[512,512]{1,0:T(8,128)(2,1)} %constant.15.clone.low_ref) | copy-start | bytes 1572868
  50.8 42.6 %copy-start.1 = (bf16[512,512]{1,0:T(8,128)(2,1)S(1)}, bf16[512,512]{1,0:T(8,128)(2,1)}, u32[]{:S(2)}) copy-start(bf16[512,512]{1,0:T(8,128)(2,1)} %constant.14.clone.high_ref) | copy-start | bytes 1572868
  50.9 42.5 %copy-start.5 = (f32[16,256]{1,0:T(8,128)S(1)}, f32[16,256]{1,0:T(8,128)}, u32[]{:S(2)}) copy-start(f32[16,256]{1,0:T(8,128)} %constant.16.clone.mix_ref) | copy-start | bytes 49156
